TPU v7x, 32 devices: a whole 2x2x4 slice. The times are simulated.
32 devices in a mesh: pipe: 4 (over x, core), ctx: 8 (over z, y).
Axes of the slice: x: 2, y: 2, z: 4, core: 2. Of those that a mesh axis runs over, the one named last changes fastest.
Arguments:
- queries: bfloat16 [2, 4, 1024, 2560], P(None, 'pipe', 'ctx'), may hold values from -80 to 80
- keys: bfloat16 [2, 4, 1024, 512], P(None, 'pipe', 'ctx'), may hold values from -25 to 25
- values: bfloat16 [2, 4, 1024, 512], P(None, 'pipe', 'ctx'), may hold values from -6 to 6
- grad_a: bfloat16 [4, 1024, 2560], P('pipe', 'ctx'), may hold values from -96 to 96
- grad_b: bfloat16 [4, 1024, 2560], P('pipe', 'ctx'), may hold values from -48 to 48
- imports: int32 [2, 4, 8, 8], P(None, 'pipe'), may hold values from 0 to 1, as said below
- block_ids: int32 [2, 4, 8], P(None, 'pipe'), may hold values from 0 to 7, each once within a row
Outputs:
- dq_a: bfloat16 [4, 1024, 2560], P('pipe', 'ctx')
- dq_b: bfloat16 [4, 1024, 2560], P('pipe', 'ctx')
- kv_grads: bfloat16 [2, 4, 1024, 1024], P(None, 'pipe', 'ctx')
Inputs may be any that keep to these rules, and one draw needn't show every extreme that they name: Every file block sees itself and imports at most 7 other blocks; in each micro-batch and section some block imports exactly 7.
All inputs are finite; a program needn't handle non-finite values.
Results may differ from a plain program's by a relative error of at most 0.015.
Values may be sent and summed in bfloat16 or wider, within the bound.
No kernel may reach another device: no remote copies, remote signals or barrier semaphores. Data moves between devices by JAX's collectives and lax.ppermute only.
A program may use at most 64 MiB of HBM per device.

v0:
```python
import math

import jax
import jax.numpy as jnp
from jax import lax
from jax.sharding import PartitionSpec as P

QUERY_HEADS = 20
KEY_VALUE_HEADS = 4
HEAD_DIMENSION = 128
FILE_BLOCK_SIZE = 128
MICRO_BATCHES = 2


negative_large = -1e30


def passed_along(block, axis, distance):
    devices = range(lax.axis_size(axis))
    route = [(i - distance, i) for i in devices if i - distance in devices]
    return lax.ppermute(block, axis, route)


def slot_table(import_mask, block_order):
    blocks_all = block_order.shape[0]
    onehot = (block_order[:, None] == jnp.arange(blocks_all, dtype=jnp.int32)[None, :]).astype(
        jnp.float32
    )
    mapped = jnp.dot(onehot, import_mask.astype(jnp.float32), precision=lax.Precision.HIGHEST)
    return jnp.dot(mapped, onehot.T, precision=lax.Precision.HIGHEST)


def frame_setup(slot_mask, query_start, row_total):
    row_index = query_start + jnp.arange(row_total, dtype=jnp.int32)
    query_slots = row_index // FILE_BLOCK_SIZE
    onehot = (
        query_slots[:, None] == jnp.arange(slot_mask.shape[0], dtype=jnp.int32)[None, :]
    ).astype(jnp.float32)
    reachable = jnp.dot(onehot, slot_mask, precision=lax.Precision.HIGHEST)
    return (reachable, query_slots, row_index % FILE_BLOCK_SIZE)


def tile_mask(frame_info, key_start, key_total_count):
    reachable, query_slots, query_place = frame_info
    key_index = key_start + jnp.arange(key_total_count, dtype=jnp.int32)
    key_slots = key_index // FILE_BLOCK_SIZE
    onehot_keys = (
        key_slots[:, None] == jnp.arange(reachable.shape[1], dtype=jnp.int32)[None, :]
    ).astype(jnp.float32)
    allowed_slot = jnp.dot(reachable, onehot_keys.T, precision=lax.Precision.HIGHEST) > 0.5
    same_slot = query_slots[:, None] == key_slots[None, :]
    causal = (key_index % FILE_BLOCK_SIZE)[None, :] <= query_place[:, None]
    return allowed_slot & (jnp.logical_not(same_slot) | causal)


def over_piece(step_fn, carried, pieces):
    key_fragment, value_fragment = pieces
    piece_rows = key_fragment.shape[0]

    def loop_turn(turn_index, carry_state):
        key_block = lax.dynamic_slice_in_dim(
            key_fragment, turn_index * FILE_BLOCK_SIZE, FILE_BLOCK_SIZE, 0
        )
        value_block = lax.dynamic_slice_in_dim(
            value_fragment, turn_index * FILE_BLOCK_SIZE, FILE_BLOCK_SIZE, 0
        )
        return step_fn(carry_state, key_block, value_block, turn_index * FILE_BLOCK_SIZE)

    return lax.fori_loop(0, piece_rows // FILE_BLOCK_SIZE, loop_turn, carried)


def micro_pass(query_row_tensor, key_rows, value_rows, incoming_gradient, slot_mask, query_start):
    row_total = query_row_tensor.shape[0]
    query_group_width = QUERY_HEADS // KEY_VALUE_HEADS
    softmax_scale = 1.0 / math.sqrt(HEAD_DIMENSION)
    query_head_tensor = query_row_tensor.reshape(
        row_total, KEY_VALUE_HEADS, query_group_width, HEAD_DIMENSION
    )
    gradient_heads = incoming_gradient.reshape(
        row_total, KEY_VALUE_HEADS, query_group_width, HEAD_DIMENSION
    )
    frame_info = frame_setup(slot_mask, query_start, row_total)
    overall_rows = slot_mask.shape[0] * FILE_BLOCK_SIZE

    def stat_step(carried, key_fragment, value_fragment, key_start):
        key_total_count = key_fragment.shape[0]
        allowed = tile_mask(frame_info, key_start, key_total_count)

        def stat_compute_tile(carry_state):
            running_max, running_sum, weighted = carry_state
            key_head_tensor = key_fragment.reshape(key_total_count, KEY_VALUE_HEADS, HEAD_DIMENSION)
            value_head_tensor = value_fragment.reshape(
                key_total_count, KEY_VALUE_HEADS, HEAD_DIMENSION
            )
            scores = (
                jnp.einsum(
                    "rhgd,khd->hgrk",
                    query_head_tensor,
                    key_head_tensor,
                    preferred_element_type=jnp.float32,
                )
                * softmax_scale
            )
            masked = jnp.where(allowed, scores, negative_large)
            new_max = jnp.maximum(running_max, jnp.max(masked, axis=-1))
            weights = jnp.where(allowed, jnp.exp(masked - new_max[..., None]), 0.0)
            rescale = jnp.exp(running_max - new_max)
            running_sum = running_sum * rescale + jnp.sum(weights, axis=-1)
            added = jnp.einsum(
                "hgrk,khd->rhgd",
                weights.astype(jnp.bfloat16),
                value_head_tensor,
                preferred_element_type=jnp.float32,
            )
            weighted = weighted * jnp.transpose(rescale, (2, 0, 1))[..., None] + added
            return (new_max, running_sum, weighted)

        return lax.cond(
            jnp.any(allowed), stat_compute_tile, lambda carry_state: carry_state, carried
        )

    stat_start = (
        jnp.full((KEY_VALUE_HEADS, query_group_width, row_total), negative_large, jnp.float32),
        jnp.zeros((KEY_VALUE_HEADS, query_group_width, row_total), jnp.float32),
        jnp.zeros((row_total, KEY_VALUE_HEADS, query_group_width, HEAD_DIMENSION), jnp.float32),
    )
    stats = over_piece(
        stat_step,
        stat_start,
        (
            lax.all_gather(key_rows, "ctx", axis=0, tiled=True),
            lax.all_gather(value_rows, "ctx", axis=0, tiled=True),
        ),
    )
    running_max, running_sum, weighted = stats
    attended = weighted / jnp.transpose(running_sum, (2, 0, 1))[..., None]
    log_total = running_max + jnp.log(running_sum)
    delta = jnp.transpose(
        jnp.sum(gradient_heads.astype(jnp.float32) * attended, axis=-1), (1, 2, 0)
    )

    def grad_step(carried, key_fragment, value_fragment, key_start):
        key_total_count = key_fragment.shape[0]
        allowed = tile_mask(frame_info, key_start, key_total_count)

        def grad_compute_tile(carry_state):
            q_grad, kv_sums = carry_state
            key_head_tensor = key_fragment.reshape(key_total_count, KEY_VALUE_HEADS, HEAD_DIMENSION)
            value_head_tensor = value_fragment.reshape(
                key_total_count, KEY_VALUE_HEADS, HEAD_DIMENSION
            )
            scores = (
                jnp.einsum(
                    "rhgd,khd->hgrk",
                    query_head_tensor,
                    key_head_tensor,
                    preferred_element_type=jnp.float32,
                )
                * softmax_scale
            )
            probs = jnp.where(
                allowed,
                jnp.exp(jnp.where(allowed, scores - log_total[..., None], negative_large)),
                0.0,
            )
            value_gradient = jnp.einsum(
                "hgrk,rhgd->khd",
                probs.astype(jnp.bfloat16),
                gradient_heads,
                preferred_element_type=jnp.float32,
            )
            prob_grad = jnp.einsum(
                "rhgd,khd->hgrk",
                gradient_heads,
                value_head_tensor,
                preferred_element_type=jnp.float32,
            )
            score_grad = (probs * (prob_grad - delta[..., None])).astype(jnp.bfloat16)
            q_grad = q_grad + jnp.einsum(
                "hgrk,khd->rhgd", score_grad, key_head_tensor, preferred_element_type=jnp.float32
            )
            key_gradient = (
                jnp.einsum(
                    "hgrk,rhgd->khd",
                    score_grad,
                    query_head_tensor,
                    preferred_element_type=jnp.float32,
                )
                * softmax_scale
            )
            update_rows = jnp.concatenate(
                [
                    key_gradient.reshape(key_total_count, KEY_VALUE_HEADS * HEAD_DIMENSION),
                    value_gradient.reshape(key_total_count, KEY_VALUE_HEADS * HEAD_DIMENSION),
                ],
                axis=1,
            )
            previous = lax.dynamic_slice_in_dim(kv_sums, key_start, key_total_count, 0)
            kv_sums = lax.dynamic_update_slice_in_dim(kv_sums, previous + update_rows, key_start, 0)
            return (q_grad, kv_sums)

        return lax.cond(
            jnp.any(allowed), grad_compute_tile, lambda carry_state: carry_state, carried
        )

    grad_start = (
        jnp.zeros((row_total, KEY_VALUE_HEADS, query_group_width, HEAD_DIMENSION), jnp.float32),
        jnp.zeros((overall_rows, 2 * KEY_VALUE_HEADS * HEAD_DIMENSION), jnp.float32),
    )
    q_grad, kv_sums = over_piece(
        grad_step,
        grad_start,
        (
            lax.all_gather(key_rows, "ctx", axis=0, tiled=True),
            lax.all_gather(value_rows, "ctx", axis=0, tiled=True),
        ),
    )
    returned = lax.psum_scatter(
        kv_sums.astype(jnp.bfloat16), "ctx", scatter_dimension=0, tiled=True
    )
    q_result = (
        (q_grad * softmax_scale)
        .reshape(row_total, QUERY_HEADS * HEAD_DIMENSION)
        .astype(jnp.bfloat16)
    )
    return (q_result, returned)


def on_device(queries, keys, values, grad_a, grad_b, imports, block_ids):
    row_total = queries.shape[2]
    query_start = lax.axis_index("ctx") * row_total
    outputs = []
    kv_results = []
    incoming_gradient = grad_a[0]
    for micro_index in range(MICRO_BATCHES):
        if micro_index > 0:
            arrived = passed_along(outputs[0], "pipe", -1)
            incoming_gradient = (
                grad_b[0].astype(jnp.float32) + arrived.astype(jnp.float32)
            ).astype(jnp.bfloat16)
        slot_mask = slot_table(imports[micro_index, 0], block_ids[micro_index, 0])
        q_result, kv_result = micro_pass(
            queries[micro_index, 0],
            keys[micro_index, 0],
            values[micro_index, 0],
            incoming_gradient,
            slot_mask,
            query_start,
        )
        outputs.append(q_result)
        kv_results.append(kv_result)
    return (outputs[0][None], outputs[1][None], jnp.stack(kv_results)[:, None])


def solution(mesh):
    return jax.shard_map(
        on_device,
        mesh=mesh,
        in_specs=(
            P(None, "pipe", "ctx", None),
            P(None, "pipe", "ctx", None),
            P(None, "pipe", "ctx", None),
            P("pipe", "ctx", None),
            P("pipe", "ctx", None),
            P(None, "pipe", None, None),
            P(None, "pipe", None),
        ),
        out_specs=(P("pipe", "ctx", None), P("pipe", "ctx", None), P(None, "pipe", "ctx", None)),
        check_vma=False,
    )
```

profile of v0, /device:TPU:0, one launch (start us, length us, event | category | flops | bytes accessed | tf_op | source)
XLA Modules:
  0.0 387.5 jit_solution(14449875247512819807)
XLA Ops:
  7.2 1.1 fusion.103
  13.5 1.1 copy.59
  16.2 1.1 copy.66
  17.3 1.2 copy.67
  18.5 34.5 %all-gather.9.cloned.1.call-done = bf16[1,1,1024,512]{2,3,1,0:T(8,128)(2,1)} async-done(((bf16[1,1,128,512]{2,3,1,0:T(8,128)(2,1)}), bf16[1,1,1024,512]{2,3,1,0:T(8,128)(2,1)}) %all-gather.9.cloned.1.call-update) | async-done | bytes 1048592 | tf_op jit(solution)/shard_map/all_gather | solution.py:214
  52.9 40.5 %all-gather.11.cloned.1.call-done = bf16[1,1,1024,512]{2,3,1,0:T(8,128)(2,1)} async-done(((bf16[1,1,128,512]{2,3,1,0:T(8,128)(2,1)}), bf16[1,1,1024,512]{2,3,1,0:T(8,128)(2,1)}) %all-gather.11.cloned.1.call-update) | async-done | bytes 1048592 | tf_op jit(solution)/shard_map/all_gather | solution.py:215
  93.6 39.7 %while.80 = (s32[]{:T(128)}, f32[4,5,128]{2,1,0:T(8,128)S(1)}, f32[4,5,128]{2,1,0:T(8,128)S(1)}, f32[128,4,5,128]{3,0,2,1:T(8,128)S(1)}, f32[128,8]{0,1:T(8,128)...) while((s32[]{:T(128)}, f32[4,5,128]{2,1,0:T(8,128)S(1)}, ...), condition=%wide.region_6.7_spmd.clone.clone, body=%wide.region_0.6_spmd.clone.clone.sunk | while | flops 173078016 | bytes 8233261 | solution.py:69
  95.2 3.7 conditional.16
  96.3 1.5 fusion.95
  100.7 3.7 conditional.16
  100.7 1.0 constant_dynamic-slice_fusion
  101.7 1.5 fusion.95
  106.1 3.7 conditional.16
  106.1 1.0 constant_dynamic-slice_fusion
  107.1 1.5 fusion.95
  111.5 3.7 conditional.16
  111.6 1.0 constant_dynamic-slice_fusion
  112.6 1.5 fusion.95
  118.7 3.8 conditional.16
  118.7 1.0 constant_dynamic-slice_fusion
  119.7 1.5 fusion.95
  124.1 3.7 conditional.16
  124.2 1.0 constant_dynamic-slice_fusion
  125.2 1.5 fusion.95
  129.6 3.7 conditional.16
  130.6 1.5 fusion.95
  133.3 1.5 copy.61
  134.8 1.5 multiply_reduce_fusion.1
  136.5 2.5 broadcast.931.clone
  139.0 48.9 %while.81 = (s32[]{:T(128)}, f32[128,4,5,128]{3,0,2,1:T(8,128)S(1)}, f32[1024,1024]{0,1:T(8,128)}, f32[128,8]{0,1:T(8,128)S(1)}, bf16[1024,512]{0,1:T(8,128)(2,1...) while((s32[]{:T(128)}, ...), condition=%wide.region_12.13_spmd.clone.clone, body=%wide.region_8.12_spmd.clone.clone.sunk | while | flops 424400896 | bytes 14217537 | solution.py:69
  140.5 5.2 %conditional.17 = ((f32[128,4,5,128]{3,0,2,1:T(8,128)S(1)}, f32[1024,1024]{0,1:T(8,128)})) conditional(s32[]{:T(128)} %convert_element_type.212, (f32[128,4,5,128]{3,0,2,1:T(8,128)S(1)}, f32[1024,1024]{0,1:T(8,128)}) %tuple.292, (pred[128,128]{0,1:T(8,128)(4,1)S(1)}, s32[]{:T(128)}, bf16[1024,512]{0,1:T(8,128)(2,1)}, ...), branch_computations={%region_10.10_spmd, %region_11.11_spmd} | conditional | flops 422707200 | bytes 14192706 | solution.py:202
  140.5 1.0 constant_dynamic-slice_fusion.2
  143.8 1.9 fusion.39
  147.3 5.2 %conditional.17 = ((f32[128,4,5,128]{3,0,2,1:T(8,128)S(1)}, f32[1024,1024]{0,1:T(8,128)})) conditional(s32[]{:T(128)} %convert_element_type.212, (f32[128,4,5,128]{3,0,2,1:T(8,128)S(1)}, f32[1024,1024]{0,1:T(8,128)}) %tuple.292, (pred[128,128]{0,1:T(8,128)(4,1)S(1)}, s32[]{:T(128)}, bf16[1024,512]{0,1:T(8,128)(2,1)}, ...), branch_computations={%region_10.10_spmd, %region_11.11_spmd} | conditional | flops 422707200 | bytes 14192706 | solution.py:202
  147.3 1.0 constant_dynamic-slice_fusion.2
  150.5 1.9 fusion.39
  154.0 5.2 %conditional.17 = ((f32[128,4,5,128]{3,0,2,1:T(8,128)S(1)}, f32[1024,1024]{0,1:T(8,128)})) conditional(s32[]{:T(128)} %convert_element_type.212, (f32[128,4,5,128]{3,0,2,1:T(8,128)S(1)}, f32[1024,1024]{0,1:T(8,128)}) %tuple.292, (pred[128,128]{0,1:T(8,128)(4,1)S(1)}, s32[]{:T(128)}, bf16[1024,512]{0,1:T(8,128)(2,1)}, ...), branch_computations={%region_10.10_spmd, %region_11.11_spmd} | conditional | flops 422707200 | bytes 14192706 | solution.py:202
  154.1 1.0 constant_dynamic-slice_fusion.2
  157.3 1.9 fusion.39
  160.8 5.2 %conditional.17 = ((f32[128,4,5,128]{3,0,2,1:T(8,128)S(1)}, f32[1024,1024]{0,1:T(8,128)})) conditional(s32[]{:T(128)} %convert_element_type.212, (f32[128,4,5,128]{3,0,2,1:T(8,128)S(1)}, f32[1024,1024]{0,1:T(8,128)}) %tuple.292, (pred[128,128]{0,1:T(8,128)(4,1)S(1)}, s32[]{:T(128)}, bf16[1024,512]{0,1:T(8,128)(2,1)}, ...), branch_computations={%region_10.10_spmd, %region_11.11_spmd} | conditional | flops 422707200 | bytes 14192706 | solution.py:202
  164.0 1.9 fusion.39
  169.1 5.2 %conditional.17 = ((f32[128,4,5,128]{3,0,2,1:T(8,128)S(1)}, f32[1024,1024]{0,1:T(8,128)})) conditional(s32[]{:T(128)} %convert_element_type.212, (f32[128,4,5,128]{3,0,2,1:T(8,128)S(1)}, f32[1024,1024]{0,1:T(8,128)}) %tuple.292, (pred[128,128]{0,1:T(8,128)(4,1)S(1)}, s32[]{:T(128)}, bf16[1024,512]{0,1:T(8,128)(2,1)}, ...), branch_computations={%region_10.10_spmd, %region_11.11_spmd} | conditional | flops 422707200 | bytes 14192706 | solution.py:202
  172.4 1.9 fusion.39
  175.9 5.2 %conditional.17 = ((f32[128,4,5,128]{3,0,2,1:T(8,128)S(1)}, f32[1024,1024]{0,1:T(8,128)})) conditional(s32[]{:T(128)} %convert_element_type.212, (f32[128,4,5,128]{3,0,2,1:T(8,128)S(1)}, f32[1024,1024]{0,1:T(8,128)}) %tuple.292, (pred[128,128]{0,1:T(8,128)(4,1)S(1)}, s32[]{:T(128)}, bf16[1024,512]{0,1:T(8,128)(2,1)}, ...), branch_computations={%region_10.10_spmd, %region_11.11_spmd} | conditional | flops 422707200 | bytes 14192706 | solution.py:202
  179.2 1.9 fusion.39
  182.6 5.2 %conditional.17 = ((f32[128,4,5,128]{3,0,2,1:T(8,128)S(1)}, f32[1024,1024]{0,1:T(8,128)})) conditional(s32[]{:T(128)} %convert_element_type.212, (f32[128,4,5,128]{3,0,2,1:T(8,128)S(1)}, f32[1024,1024]{0,1:T(8,128)}) %tuple.292, (pred[128,128]{0,1:T(8,128)(4,1)S(1)}, s32[]{:T(128)}, bf16[1024,512]{0,1:T(8,128)(2,1)}, ...), branch_computations={%region_10.10_spmd, %region_11.11_spmd} | conditional | flops 422707200 | bytes 14192706 | solution.py:202
  185.9 1.9 fusion.39
  187.9 1.5 copy.62
  189.4 2.4 multiply_convert_fusion.1
  191.8 1.3 collective-permute-start
  193.3 15.4 %while.82 = (s32[]{:T(128)}, f32[4,5,128]{2,1,0:T(8,128)S(1)}, f32[4,5,128]{2,1,0:T(8,128)S(1)}, f32[128,4,5,128]{3,0,2,1:T(8,128)S(1)}, f32[128,8]{0,1:T(8,128)...) while((s32[]{:T(128)}, f32[4,5,128]{2,1,0:T(8,128)S(1)}, ...), condition=%wide.region_19.20_spmd.clone.clone, body=%wide.region_13.0_spmd.clone.clone.sunk | while | flops 173078016 | bytes 8233261 | solution.py:69
  194.9 2.6 conditional.18
  209.1 4.6 %copy.70 = bf16[1024,1024]{1,0:T(8,128)(2,1)} copy(f32[1024,1024]{0,1:T(8,128)} %get-tuple-element.1589) | data formatting | bytes 6291456 | tf_op jit(solution)/shard_map/while | solution.py:69
  214.8 1.3 fusion.76
  216.4 2.5 broadcast.931
  218.9 17.9 %while.83 = (s32[]{:T(128)}, f32[128,4,5,128]{3,0,2,1:T(8,128)S(1)}, f32[1024,1024]{0,1:T(8,128)}, f32[128,8]{0,1:T(8,128)S(1)}, bf16[1024,512]{0,1:T(8,128)(2,1...) while((s32[]{:T(128)}, ...), condition=%wide.region_25.26_spmd.clone.clone, body=%wide.region_21.25_spmd.clone.clone.sunk | while | flops 424400896 | bytes 14217537 | solution.py:69
  220.5 5.2 %conditional.19 = ((f32[128,4,5,128]{3,0,2,1:T(8,128)S(1)}, f32[1024,1024]{0,1:T(8,128)})) conditional(s32[]{:T(128)} %convert_element_type.214, (f32[128,4,5,128]{3,0,2,1:T(8,128)S(1)}, f32[1024,1024]{0,1:T(8,128)}) %tuple.304, (pred[128,128]{0,1:T(8,128)(4,1)S(1)}, s32[]{:T(128)}, bf16[1024,512]{0,1:T(8,128)(2,1)}, ...), branch_computations={%region_23.23_spmd, %region_24.24_spmd} | conditional | flops 422707200 | bytes 14192706 | solution.py:202
  223.8 1.9 fusion.63
  236.8 4.7 %copy.71 = bf16[1024,1024]{1,0:T(8,128)(2,1)} copy(f32[1024,1024]{0,1:T(8,128)} %get-tuple-element.1590) | data formatting | bytes 6291456 | tf_op jit(solution)/shard_map/while | solution.py:69
  241.5 2.2 copy.72
  244.3 1.1 copy.73
  245.4 63.1 %reduce-scatter.3.cloned.1.call-done = bf16[128,1024]{1,0:T(8,128)(2,1)} async-done(((bf16[1024,1024]{1,0:T(8,128)(2,1)}), bf16[128,1024]{1,0:T(8,128)(2,1)}) %reduce-scatter.3.cloned.1.call-update) | async-done | bytes 262160 | tf_op jit(solution)/shard_map/reduce_scatter | solution.py:218
  308.5 70.2 %reduce-scatter.5.cloned.1.call-done = bf16[128,1024]{1,0:T(8,128)(2,1)} async-done(((bf16[1024,1024]{1,0:T(8,128)(2,1)}), bf16[128,1024]{1,0:T(8,128)(2,1)}) %reduce-scatter.5.cloned.1.call-update) | async-done | bytes 262160 | tf_op jit(solution)/shard_map/reduce_scatter | solution.py:218
  378.8 1.9 maximum_bitcast_fusion
  (261 shorter events, 74.0 us)
Async XLA Ops:
  7.2 5.5 %copy-start.5 = (s32[2,1,8]{2,1,0:T(1,128)S(1)}, s32[2,1,8]{2,1,0:T(1,128)}, u32[]{:S(2)}) copy-start(s32[2,1,8]{2,1,0:T(1,128)} %param.29) | copy-start | bytes 196
  7.2 5.5 %copy-start.6 = (s32[2,1,8,8]{3,2,1,0:T(8,128)S(1)}, s32[2,1,8,8]{3,2,1,0:T(8,128)}, u32[]{:S(2)}) copy-start(s32[2,1,8,8]{3,2,1,0:T(8,128)} %param.28) | copy-start | bytes 1540
  7.2 5.9 %copy-start.2 = (bf16[2,1,128,2560]{3,2,1,0:T(8,128)(2,1)S(1)}, bf16[2,1,128,2560]{3,2,1,0:T(8,128)(2,1)}, u32[]{:S(2)}) copy-start(bf16[2,1,128,2560]{3,2,1,0:T(8,128)(2,1)} %param.23) | copy-start | bytes 3932164
  7.2 45.7 %all-gather.9.cloned.1.call-start = ((), (), s32[]{:S(2)}) async-start(), calls=%async_computation.4 | async-start | bytes 1179648 | tf_op jit(solution)/shard_map/all_gather | solution.py:214
  9.1 84.3 %all-gather.11.cloned.1.call-start = ((), (), s32[]{:S(2)}) async-start(), calls=%async_computation.5 | async-start | bytes 1179648 | tf_op jit(solution)/shard_map/all_gather | solution.py:215
  10.9 182.1 %all-gather.13.cloned.1.call-start = ((), (), s32[]{:S(2)}) async-start(), calls=%async_computation.6 | async-start | bytes 1179648 | tf_op jit(solution)/shard_map/all_gather | solution.py:214
  11.8 181.3 %all-gather.15.cloned.1.call-start = ((), (), s32[]{:S(2)}) async-start(), calls=%async_computation.7 | async-start | bytes 1179648 | tf_op jit(solution)/shard_map/all_gather | solution.py:215
  12.6 295.9 %reduce-scatter.3.cloned.1.call-start = ((), (), s32[]{:S(2)}) async-start(), calls=%async_computation.2 | async-start | bytes 2359296 | tf_op jit(solution)/shard_map/reduce_scatter | solution.py:218
  13.2 1.4 copy-start.3
  15.8 1.5 copy-start.4
  189.4 3.9 %copy-start = (bf16[128,4,5,128]{3,0,2,1:T(8,128)(2,1)S(1)}, bf16[128,4,5,128]{3,0,2,1:T(8,128)(2,1)}, u32[]{:S(2)}) copy-start(bf16[128,4,5,128]{3,0,2,1:T(8,128)(2,1)} %copy.66) | copy-start | bytes 1966084
  191.8 22.2 %collective-permute-start = (bf16[128,2560]{0,1:T(8,128)(2,1)}, bf16[128,2560]{0,1:T(8,128)(2,1)}, u32[]{:S(2)}, u32[]{:S(2)}) collective-permute-start(bf16[128,2560]{0,1:T(8,128)(2,1)} %bitcast.61), channel_id=1, source_target_pairs={{8,0},{16,8},{24,16},{9,1},{17,9},{25,17},{10,2},{18,10},{26,18},{... | collective-permute-start | bytes 1966088 | tf_op jit(solution)/shard_map/ppermute | solution.py:21
  213.7 1.1 copy-start.1
  213.8 165.0 %reduce-scatter.5.cloned.1.call-start = ((), (), s32[]{:S(2)}) async-start(), calls=%async_computation.3 | async-start | bytes 2359296 | tf_op jit(solution)/shard_map/reduce_scatter | solution.py:218
Sparse Core Ops, SparseCore 0:
  10.6 42.2 all-gather.8
  55.0 38.4 all-gather.10
  95.5 39.0 all-gather.12
  136.5 37.7 all-gather.14
  213.9 94.5 reduce-scatter.2
  311.9 66.8 reduce-scatter.4
where the time goes:
time: 385 us; the launch traced here: 387 us
  waiting for transfers between devices  208 us (54%)
  matrix products  65.3 us (17%)
  local copies, waits for them, and re-layouts  48.2 us (13%)
  other arithmetic  25.8 us (7%)
  loops' own time  23.5 us (6%)
  between operations  14.4 us (4%)
    reduce_scatter x2, waiting for transfers between devices, micro_pass(): lax.psum_scatter(kv_sums.astype(jnp.bfloat16), 'ctx', scatter_dimension=0...  133 us
    all_gather x2, waiting for transfers between devices, micro_pass(): lax.all_gather(value_rows, 'ctx', axis=0, tiled=True)  40.5 us
    all_gather x2, waiting for transfers between devices, micro_pass(): lax.all_gather(key_rows, 'ctx', axis=0, tiled=True)  34.5 us
    dot_general x32, matrix products, tile_mask(): jnp.dot(reachable, onehot_keys.T, precision=lax.Precision.HIGHEST) > 0.5  28.3 us
    another operation x4, loops' own time, over_piece(): return lax.fori_loop(0, piece_rows // FILE_BLOCK_SIZE, loop_turn, carried)  22.2 us
    dynamic_slice x16, local copies, waits for them, and re-layouts, loop_turn(): lax.dynamic_slice_in_dim(value_fragment, turn_index * FILE_BLOCK_SIZE, FI...  16 us
    dynamic_update_slice x8, other arithmetic, grad_compute_tile(): lax.dynamic_update_slice_in_dim(kv_sums, previous + update_rows, key_star...  15.5 us
    while x6, local copies, waits for them, and re-layouts, over_piece(): return lax.fori_loop(0, piece_rows // FILE_BLOCK_SIZE, loop_turn, carried)  13.1 us
  transfers between devices with their start and end apart: 7, of which 4 were waited for; matrix products, arithmetic and copies ran while one was open for 35% of the time, Pallas kernels for 0%

commit v1 on v0

v1 whole, which is shorter than its diff:
```python
import math

import jax
import jax.numpy as jnp
from jax import lax
from jax.experimental import pallas as pl
from jax.experimental.pallas import tpu as pltpu
from jax.sharding import PartitionSpec as P

QUERY_HEADS = 20
KEY_VALUE_HEADS = 4
HEAD_DIMENSION = 128
FILE_BLOCK_SIZE = 128
MICRO_BATCHES = 2

GROUP = QUERY_HEADS // KEY_VALUE_HEADS
SIDES = 2
HALF_KV = KEY_VALUE_HEADS // SIDES
HALF_Q_WIDTH = HALF_KV * GROUP * HEAD_DIMENSION
HALF_KV_WIDTH = HALF_KV * HEAD_DIMENSION
STACK = GROUP * FILE_BLOCK_SIZE
negative_large = -1e30
SCALE = 1.0 / math.sqrt(HEAD_DIMENSION)
EXP2_SCALE = SCALE * math.log2(math.e)

NT = (((1,), (1,)), ((), ()))
NN = (((1,), (0,)), ((), ()))
TN = (((0,), (0,)), ((), ()))


def folded_order(lines):
    return [0] + list(range(1, lines, 2)) + list(range(2, lines, 2))[::-1]


def line_position(line, lines):
    odd = lax.rem(line, 2) == 1
    return jnp.where(line == 0, 0, jnp.where(odd, (line + 1) // 2, lines - line // 2))


def position_line(position, lines):
    return jnp.where(
        position == 0, 0, jnp.where(position <= lines // 2, 2 * position - 1, 2 * (lines - position))
    )


def fold_rows(tile, op):
    rows, columns = tile.shape
    return op(tile.reshape(rows // 8, 8, columns), axis=0)


def backward_kernel(lines, micro, with_arrived, *refs):
    side_count = SIDES
    tiles = lines * side_count
    refs = list(refs)
    imports_ref, ids_ref = refs[:2]
    q_refs, g_refs = refs[2:4], refs[4:6]
    at = 6
    arrived_refs = None
    if with_arrived:
        arrived_refs = refs[at : at + 2]
        at += 2
    kv_refs = refs[at : at + tiles]
    at += tiles
    dq_refs = refs[at : at + 2]
    at += 2
    dkv_refs = refs[at : at + tiles]
    at += tiles
    kv_all, q_stack, g_stack, scores, dprobs, dkv_sum, listing = refs[at:]

    me = lax.axis_index("ctx")
    line, side = me // side_count, lax.rem(me, side_count)
    position = line_position(line, lines)

    for tile in range(tiles):
        kv_all[tile] = kv_refs[tile][...]
    dkv_sum[...] = jnp.zeros_like(dkv_sum)

    for block in range(side_count):
        query_slot = line * side_count + (side if block == 0 else 1 - side)
        query_id = ids_ref[micro, 0, query_slot]
        count = jnp.int32(0)
        for step in range(lines):
            source = lax.rem(position - step + lines, lines)
            key_line = position_line(source, lines)
            for chain in range(side_count):
                if step == 0 and chain == block:
                    continue
                key_slot = key_line * side_count + (side if chain == 0 else 1 - side)
                key_id = ids_ref[micro, 0, key_slot]
                listing[block, count] = step * side_count + chain
                count = count + jnp.where(imports_ref[micro, 0, query_id, key_id] > 0, 1, 0)
        listing[block, tiles] = count

    triangle = lax.broadcasted_iota(jnp.int32, (FILE_BLOCK_SIZE, FILE_BLOCK_SIZE), 0) <= (
        lax.broadcasted_iota(jnp.int32, (FILE_BLOCK_SIZE, FILE_BLOCK_SIZE), 1)
    )
    allowed = jnp.concatenate([triangle] * GROUP, axis=1)

    for block in range(side_count):
        count = listing[block, tiles]
        for head in range(HALF_KV):
            for member in range(GROUP):
                rows = slice(member * FILE_BLOCK_SIZE, (member + 1) * FILE_BLOCK_SIZE)
                start = (head * GROUP + member) * HEAD_DIMENSION
                columns = slice(start, start + HEAD_DIMENSION)
                q_stack[rows, :] = q_refs[block][:, columns]
                upstream = g_refs[block][:, columns]
                if with_arrived:
                    upstream = (
                        upstream.astype(jnp.float32)
                        + arrived_refs[block][:, columns].astype(jnp.float32)
                    ).astype(jnp.bfloat16)
                g_stack[rows, :] = upstream
            key_columns = slice(head * HEAD_DIMENSION, (head + 1) * HEAD_DIMENSION)
            value_columns = slice(
                HALF_KV_WIDTH + head * HEAD_DIMENSION, HALF_KV_WIDTH + (head + 1) * HEAD_DIMENSION
            )

            def products(tile):
                score = lax.dot_general(
                    kv_all[tile, :, key_columns],
                    q_stack[...],
                    NT,
                    preferred_element_type=jnp.float32,
                )
                dprobs[tile] = lax.dot_general(
                    kv_all[tile, :, value_columns],
                    g_stack[...],
                    NT,
                    preferred_element_type=jnp.float32,
                )
                return score

            own = block
            score = jnp.where(allowed, products(own), negative_large)
            scores[own] = score

            def first(turn, largest):
                tile = listing[block, turn]
                score = products(tile)
                scores[tile] = score
                return jnp.maximum(largest, fold_rows(score, jnp.max))

            largest = lax.fori_loop(0, count, first, fold_rows(score, jnp.max))
            row_max = jnp.max(largest, axis=0, keepdims=True)

            def weigh(tile):
                weight = jnp.exp2((scores[tile] - row_max) * EXP2_SCALE)
                scores[tile] = weight
                return fold_rows(weight, jnp.sum), fold_rows(weight * dprobs[tile], jnp.sum)

            def second(turn, sums):
                added = weigh(listing[block, turn])
                return (sums[0] + added[0], sums[1] + added[1])

            sums = lax.fori_loop(0, count, second, weigh(own))
            inverse = 1.0 / jnp.sum(sums[0], axis=0, keepdims=True)
            delta = jnp.sum(sums[1], axis=0, keepdims=True) * inverse

            def spread(tile):
                prob = scores[tile] * inverse
                score_grad = (prob * (dprobs[tile] - delta)).astype(jnp.bfloat16)
                dkv_sum[tile, :, key_columns] += lax.dot_general(
                    score_grad, q_stack[...], NN, preferred_element_type=jnp.float32
                )
                dkv_sum[tile, :, value_columns] += lax.dot_general(
                    prob.astype(jnp.bfloat16), g_stack[...], NN, preferred_element_type=jnp.float32
                )
                return lax.dot_general(
                    kv_all[tile, :, key_columns], score_grad, TN, preferred_element_type=jnp.float32
                )

            def third(turn, total):
                return total + spread(listing[block, turn])

            dq_turned = lax.fori_loop(0, count, third, spread(own)) * SCALE
            for member in range(GROUP):
                start = (head * GROUP + member) * HEAD_DIMENSION
                part = dq_turned[:, member * FILE_BLOCK_SIZE : (member + 1) * FILE_BLOCK_SIZE]
                dq_refs[block][:, start : start + HEAD_DIMENSION] = part.T.astype(jnp.bfloat16)

    for tile in range(tiles):
        dkv_refs[tile][:, :HALF_KV_WIDTH] = (dkv_sum[tile, :, :HALF_KV_WIDTH] * SCALE).astype(
            jnp.bfloat16
        )
        dkv_refs[tile][:, HALF_KV_WIDTH:] = dkv_sum[tile, :, HALF_KV_WIDTH:].astype(jnp.bfloat16)


def backward(lines, micro, imports, block_ids, q_pair, g_pair, arrived_pair, kv_tiles):
    tiles = lines * SIDES
    with_arrived = arrived_pair is not None
    vmem = pl.BlockSpec(memory_space=pltpu.VMEM)
    smem = pl.BlockSpec(memory_space=pltpu.SMEM)
    operands = [imports, block_ids, *q_pair, *g_pair]
    if with_arrived:
        operands += arrived_pair
    operands += kv_tiles
    query_shape = jax.ShapeDtypeStruct((FILE_BLOCK_SIZE, HALF_Q_WIDTH), jnp.bfloat16)
    key_shape = jax.ShapeDtypeStruct((FILE_BLOCK_SIZE, 2 * HALF_KV_WIDTH), jnp.bfloat16)

    def body(*refs):
        backward_kernel(lines, micro, with_arrived, *refs)

    results = pl.pallas_call(
        body,
        out_shape=[query_shape] * 2 + [key_shape] * tiles,
        in_specs=[smem, smem] + [vmem] * (len(operands) - 2),
        out_specs=[vmem] * (2 + tiles),
        scratch_shapes=[
            pltpu.VMEM((tiles, FILE_BLOCK_SIZE, 2 * HALF_KV_WIDTH), jnp.bfloat16),
            pltpu.VMEM((STACK, HEAD_DIMENSION), jnp.bfloat16),
            pltpu.VMEM((STACK, HEAD_DIMENSION), jnp.bfloat16),
            pltpu.VMEM((tiles, FILE_BLOCK_SIZE, STACK), jnp.float32),
            pltpu.VMEM((tiles, FILE_BLOCK_SIZE, STACK), jnp.float32),
            pltpu.VMEM((tiles, FILE_BLOCK_SIZE, 2 * HALF_KV_WIDTH), jnp.float32),
            pltpu.SMEM((SIDES, tiles + 1), jnp.int32),
        ],
        compiler_params=pltpu.CompilerParams(vmem_limit_bytes=48 * 1024 * 1024),
        cost_estimate=pl.CostEstimate(flops=4 * 10**9, bytes_accessed=4 * 10**6, transcendentals=0),
    )(*operands)
    return results[:2], results[2:]


def on_device(queries, keys, values, grad_a, grad_b, imports, block_ids):
    devices = lax.axis_size("ctx")
    lines = devices // SIDES
    side = lax.rem(lax.axis_index("ctx"), SIDES)
    order = folded_order(lines)
    ring = [
        (order[i] * SIDES + s, order[(i + 1) % lines] * SIDES + s)
        for i in range(lines)
        for s in range(SIDES)
    ]
    pairs = [(i, i ^ 1) for i in range(devices)]
    pipe = lax.axis_size("pipe")
    back = [(i + 1, i) for i in range(pipe - 1)]

    def swap(block):
        return lax.ppermute(block, "ctx", pairs)

    def turn(block):
        return lax.ppermute(block, "ctx", ring)

    def split(rows, width):
        kept = lax.dynamic_slice_in_dim(rows, side * width, width, 1)
        given = lax.dynamic_slice_in_dim(rows, (1 - side) * width, width, 1)
        return kept, given

    def joined(kept, received):
        ordered = jnp.concatenate([kept, received], axis=1)
        crossed = jnp.concatenate([received, kept], axis=1)
        return jnp.where(side == 0, ordered, crossed)

    def gathered(micro):
        key_kept, key_given = split(keys[micro, 0], HALF_KV_WIDTH)
        value_kept, value_given = split(values[micro, 0], HALF_KV_WIDTH)
        own = jnp.concatenate([key_kept, value_kept], axis=1)
        other = swap(jnp.concatenate([key_given, value_given], axis=1))
        tiles = [own, other]
        for _ in range(1, lines):
            own, other = turn(own), turn(other)
            tiles += [own, other]
        return tiles

    def exchanged(rows):
        kept, given = split(rows, HALF_Q_WIDTH)
        return [kept, swap(given)]

    def scattered(parts):
        sums = []
        for chain in range(SIDES):
            total = parts[SIDES + chain] if lines > 1 else parts[chain]
            for step in list(range(2, lines)) + ([0] if lines > 1 else []):
                total = (
                    turn(total).astype(jnp.float32)
                    + parts[step * SIDES + chain].astype(jnp.float32)
                ).astype(jnp.bfloat16)
            sums.append(total)
        received = swap(sums[1])
        key_part = joined(sums[0][:, :HALF_KV_WIDTH], received[:, :HALF_KV_WIDTH])
        value_part = joined(sums[0][:, HALF_KV_WIDTH:], received[:, HALF_KV_WIDTH:])
        return jnp.concatenate([key_part, value_part], axis=1)

    tiles_a = gathered(0)
    q_a = exchanged(queries[0, 0])
    g_a = exchanged(grad_a[0])
    tiles_b = gathered(1)
    q_b = exchanged(queries[1, 0])
    g_b = exchanged(grad_b[0])

    dq_a, dkv_a = backward(lines, 0, imports, block_ids, q_a, g_a, None, tiles_a)
    arrived = [lax.ppermute(part, "pipe", back) for part in dq_a]
    dq_b, dkv_b = backward(lines, 1, imports, block_ids, q_b, g_b, arrived, tiles_b)
    out_a = joined(dq_a[0], swap(dq_a[1]))
    out_b = joined(dq_b[0], swap(dq_b[1]))
    kv = jnp.stack([scattered(dkv_a), scattered(dkv_b)])
    return (out_a[None], out_b[None], kv[:, None])


def solution(mesh):
    return jax.shard_map(
        on_device,
        mesh=mesh,
        in_specs=(
            P(None, "pipe", "ctx", None),
            P(None, "pipe", "ctx", None),
            P(None, "pipe", "ctx", None),
            P("pipe", "ctx", None),
            P("pipe", "ctx", None),
            P(None, "pipe", None, None),
            P(None, "pipe", None),
        ),
        out_specs=(P("pipe", "ctx", None), P("pipe", "ctx", None), P(None, "pipe", "ctx", None)),
        check_vma=False,
    )
```

time: 385 us -> 125 us (0.32)
  waiting for transfers between devices: 208 us -> 48.8 us
  matrix products: 65.3 us -> 0 us
  local copies, waits for them, and re-layouts: 48.2 us -> 5.1 us
  starting transfers between devices: 1.71 us -> 36 us
  Pallas kernels: 0 us -> 31.6 us
  loops' own time: 23.5 us -> 0 us
  other arithmetic: 25.8 us -> 4.35 us
  between operations: 14.4 us -> 1.04 us
    reduce_scatter x2 -> x0, waiting for transfers between devices: 133 us -> none  [micro_pass(): lax.psum_scatter(kv_sums.astype(jnp.bfloat16), 'ctx', scatter_dimension=0...]
    all_gather x4 -> x0, waiting for transfers between devices: 75 us -> none  [the longest x2 40.5 us: micro_pass(): lax.all_gather(value_rows, 'ctx', axis=0, tiled=True)]
    dot_general x94 -> x0, matrix products: 65.3 us -> none  [the longest x32 28.3 us: tile_mask(): jnp.dot(reachable, onehot_keys.T, precision=lax.Precision.HIGHEST) > 0.5]
    ppermute x1 -> x36, waiting for transfers between devices: 0.01 us -> 48.8 us  [the longest x24 35.7 us: turn(): return lax.ppermute(block, 'ctx', ring)]
    ppermute x1 -> x36, starting transfers between devices: 1.28 us -> 36 us  [the longest x24 20.4 us: turn(): return lax.ppermute(block, 'ctx', ring)]
    pallas_call x0 -> x2, Pallas kernels: none -> 31.6 us  [backward(): pl.pallas_call(body, out_shape=[query_shape] * 2 + [key_shape] * tiles, i...]
    another operation x36 -> x0, loops' own time: 23.5 us -> none  [the longest x4 22.2 us: over_piece(): return lax.fori_loop(0, piece_rows // FILE_BLOCK_SIZE, loop_turn, carried)]
    dynamic_update_slice x8 -> x0, other arithmetic: 15.5 us -> none  [grad_compute_tile(): lax.dynamic_update_slice_in_dim(kv_sums, previous + update_rows, key_star...]
  transfers between devices with their start and end apart: 7 -> 36, of which waited for: 4 -> 17; matrix products, arithmetic and copies ran while one was open for 35% -> 5% of each run, Pallas kernels for 0% -> 25%
where the time goes in v1:
time: 125 us; the launch traced here: 127 us
  waiting for transfers between devices  48.8 us (39%)
  starting transfers between devices  36 us (29%)
  Pallas kernels  31.6 us (25%)
  local copies, waits for them, and re-layouts  5.1 us (4%)
  other arithmetic  4.35 us (3%)
    ppermute x24, waiting for transfers between devices, turn(): return lax.ppermute(block, 'ctx', ring)  35.7 us
    pallas_call x2, Pallas kernels, backward(): pl.pallas_call(body, out_shape=[query_shape] * 2 + [key_shape] * tiles, i...  31.6 us
    ppermute x24, starting transfers between devices, turn(): return lax.ppermute(block, 'ctx', ring)  20.4 us
    ppermute x10, waiting for transfers between devices, swap(): return lax.ppermute(block, 'ctx', pairs)  13.2 us
    ppermute x10, starting transfers between devices, swap(): return lax.ppermute(block, 'ctx', pairs)  13 us
    ppermute x2, starting transfers between devices, on_device(): arrived = [lax.ppermute(part, 'pipe', back) for part in dq_a]  2.58 us
  transfers between devices with their start and end apart: 36, of which 17 were waited for; matrix products, arithmetic and copies ran while one was open for 5% of the time, Pallas kernels for 25%

profile of v1, /device:TPU:0, one launch (start us, length us, event | category | flops | bytes accessed | tf_op | source)
XLA Modules:
  0.0 126.9 jit_solution(16897013406020959796)
XLA Ops:
  0.6 1.0 fusion.2
  1.6 1.0 fusion.1
  2.7 3.0 %collective-permute-start.2 = (bf16[128,512]{1,0:T(8,128)(2,1)S(1)}, bf16[128,512]{1,0:T(8,128)(2,1)S(1)}, u32[]{:S(2)}, u32[]{:S(2)}) collective-permute-start(bf16[128,512]{1,0:T(8,128)(2,1)S(1)} %pad_maximum_fusion.1), channel_id=1, source_target_pairs={{0,1},{1,0},{2,3},{3,2},{4,5},{5,4},{6,7},{7,6},{8,9},{9,8},{10,11... | collective-permute-start | bytes 393224 | tf_op jit(solution)/shard_map/ppermute | solution.py:239
  5.8 1.6 %collective-permute-start.3 = (bf16[128,512]{1,0:T(8,128)(2,1)S(1)}, bf16[128,512]{1,0:T(8,128)(2,1)S(1)}, u32[]{:S(2)}, u32[]{:S(2)}) collective-permute-start(bf16[128,512]{1,0:T(8,128)(2,1)S(1)} %pad_maximum_fusion.refs_6_), channel_id=1, source_target_pairs={{0,2},{1,3},{2,6},{3,7},{6,4},{7,5},{4,0},{5,1},{8,10},{9,11},{10,... | collective-permute-start | bytes 393224 | tf_op jit(solution)/shard_map/ppermute | solution.py:242
  7.4 1.4 %fusion = (bf16[1,1,128,2560]{3,2,1,0:T(8,128)(2,1)S(1)}, bf16[1,1,128,2560]{3,2,1,0:T(8,128)(2,1)S(1)}) fusion(bf16[2,1,128,2560]{3,2,1,0:T(8,128)(2,1)} %param.7), kind=kLoop, calls=%fused_computation.41 | loop fusion | bytes 2621440 | tf_op jit(solution)/shard_map/slice | solution.py:288
  8.8 0.0 copy-start.2
  8.8 0.5 collective-permute-done.2.refs_7_
  9.2 2.2 %collective-permute-start.4 = (bf16[128,512]{1,0:T(8,128)(2,1)S(1)}, bf16[128,512]{1,0:T(8,128)(2,1)S(1)}, u32[]{:S(2)}, u32[]{:S(2)}) collective-permute-start(bf16[128,512]{1,0:T(8,128)(2,1)S(1)} %collective-permute-done.2.refs_7_), channel_id=1, source_target_pairs={{0,2},{1,3},{2,6},{3,7},{6,4},{7,5},{4,0},{5,1},{8,10},{9,11},{10,... | collective-permute-start | bytes 393224 | tf_op jit(solution)/shard_map/ppermute | solution.py:242
  11.5 0.0 copy-start
  11.5 0.0 copy-start.1
  11.5 1.2 collective-permute-start
  12.7 2.6 %collective-permute-start.5 = (bf16[128,512]{1,0:T(8,128)(2,1)S(1)}, bf16[128,512]{1,0:T(8,128)(2,1)S(1)}, u32[]{:S(2)}, u32[]{:S(2)}) collective-permute-start(bf16[128,512]{1,0:T(8,128)(2,1)S(1)} %collective-permute-done.3.refs_8_), channel_id=1, source_target_pairs={{0,2},{1,3},{2,6},{3,7},{6,4},{7,5},{4,0},{5,1},{8,10},{9,11},{10,... | collective-permute-start | bytes 393224 | tf_op jit(solution)/shard_map/ppermute | solution.py:242
  15.3 0.3 collective-permute-done.4.refs_9_
  15.6 1.5 %collective-permute-start.6 = (bf16[128,512]{1,0:T(8,128)(2,1)S(1)}, bf16[128,512]{1,0:T(8,128)(2,1)S(1)}, u32[]{:S(2)}, u32[]{:S(2)}) collective-permute-start(bf16[128,512]{1,0:T(8,128)(2,1)S(1)} %collective-permute-done.4.refs_9_), channel_id=1, source_target_pairs={{0,2},{1,3},{2,6},{3,7},{6,4},{7,5},{4,0},{5,1},{8,10},{9,11},{10,... | collective-permute-start | bytes 393224 | tf_op jit(solution)/shard_map/ppermute | solution.py:242
  17.2 1.3 %collective-permute-start.1 = (bf16[128,1280]{1,0:T(8,128)(2,1)S(1)}, bf16[128,1280]{1,0:T(8,128)(2,1)S(1)}, u32[]{:S(2)}, u32[]{:S(2)}) collective-permute-start(bf16[128,1280]{1,0:T(8,128)(2,1)S(1)} %get-tuple-element.52), channel_id=1, source_target_pairs={{0,1},{1,0},{2,3},{3,2},{4,5},{5,4},{6,7},{7,6},{8,9},{9,8},{10,11... | collective-permute-start | bytes 983048 | tf_op jit(solution)/shard_map/ppermute | solution.py:239
  18.6 0.8 collective-permute-start.14
  19.4 0.3 collective-permute-done.5.refs_10_
  19.7 3.1 %collective-permute-start.7 = (bf16[128,512]{1,0:T(8,128)(2,1)S(1)}, bf16[128,512]{1,0:T(8,128)(2,1)S(1)}, u32[]{:S(2)}, u32[]{:S(2)}) collective-permute-start(bf16[128,512]{1,0:T(8,128)(2,1)S(1)} %collective-permute-done.5.refs_10_), channel_id=1, source_target_pairs={{0,2},{1,3},{2,6},{3,7},{6,4},{7,5},{4,0},{5,1},{8,10},{9,11},{10,... | collective-permute-start | bytes 393224 | tf_op jit(solution)/shard_map/ppermute | solution.py:242
  22.8 0.6 collective-permute-start.8
  23.3 0.8 dynamic-slice_bitcast_fusion.2
  24.1 5.9 %collective-permute-done.14.refs_9_ = bf16[128,512]{1,0:T(8,128)(2,1)S(1)} collective-permute-done((bf16[128,512]{1,0:T(8,128)(2,1)S(1)}, bf16[128,512]{1,0:T(8,128)(2,1)S(1)}, u32[]{:S(2)}, u32[]{:S(2)}) %collective-permute-start.14) | collective-permute-done | bytes 131104 | tf_op jit(solution)/shard_map/ppermute | solution.py:239
  30.0 1.9 %collective-permute-start.15 = (bf16[128,512]{1,0:T(8,128)(2,1)S(1)}, bf16[128,512]{1,0:T(8,128)(2,1)S(1)}, u32[]{:S(2)}, u32[]{:S(2)}) collective-permute-start(bf16[128,512]{1,0:T(8,128)(2,1)S(1)} %pad_maximum_fusion.2.refs_8_), channel_id=1, source_target_pairs={{0,2},{1,3},{2,6},{3,7},{6,4},{7,5},{4,0},{5,1},{8,10},{9,11},{10,... | collective-permute-start | bytes 393224 | tf_op jit(solution)/shard_map/ppermute | solution.py:242
  31.9 1.5 %collective-permute-start.10 = (bf16[128,1280]{1,0:T(8,128)(2,1)}, bf16[128,1280]{1,0:T(8,128)(2,1)S(1)}, u32[]{:S(2)}, u32[]{:S(2)}) collective-permute-start(bf16[128,1280]{1,0:T(8,128)(2,1)} %get-tuple-element.50), channel_id=1, source_target_pairs={{0,1},{1,0},{2,3},{3,2},{4,5},{5,4},{6,7},{7,6},{8,9},{9,8},{10,11... | collective-permute-start | bytes 983048 | tf_op jit(solution)/shard_map/ppermute | solution.py:239
  33.4 0.0 collective-permute-done.1.refs_5_
  33.4 0.5 collective-permute-start.16
  33.9 0.0 copy-start.3
  33.9 17.0 %shard_map.94 = (bf16[128,1280]{1,0:T(8,128)(2,1)S(1)}, bf16[128,1280]{1,0:T(8,128)(2,1)S(1)}, bf16[128,512]{1,0:T(8,128)(2,1)S(1)}, bf16[128,512]{1,0:T(8,128)(...) custom-call(s32[2,1,8,8]{3,2,1,0:T(8,128)S(1)} %copy-done, ...), custom_call_target="tpu_custom_call" | custom-call | flops 4000000000 | bytes 4000000 | tf_op jit(solution)/shard_map/pallas_call | solution.py:204
  50.9 0.1 collective-permute-start.22
  51.0 0.8 dynamic-slice_bitcast_fusion
  51.8 0.5 collective-permute-start.11
  52.3 3.2 %collective-permute-start.18 = (bf16[128,512]{1,0:T(8,128)(2,1)S(1)}, bf16[128,512]{1,0:T(8,128)(2,1)S(1)}, u32[]{:S(2)}, u32[]{:S(2)}) collective-permute-start(bf16[128,512]{1,0:T(8,128)(2,1)S(1)} %collective-permute-done.16.refs_11_), channel_id=1, source_target_pairs={{0,2},{1,3},{2,6},{3,7},{6,4},{7,5},{4,0},{5,1},{8,10},{9,11},{10,... | collective-permute-start | bytes 393224 | tf_op jit(solution)/shard_map/ppermute | solution.py:242
  55.5 2.9 %collective-permute-done.22 = bf16[128,512]{1,0:T(8,128)(2,1)} collective-permute-done((bf16[128,512]{1,0:T(8,128)(2,1)S(1)}, bf16[128,512]{1,0:T(8,128)(2,1)}, u32[]{:S(2)}, u32[]{:S(2)}) %collective-permute-start.22) | collective-permute-done | bytes 131104 | tf_op jit(solution)/shard_map/ppermute | solution.py:242
  58.4 0.0 collective-permute-start.25
  58.4 0.9 add_convert_fusion.11
  59.4 4.9 %collective-permute-done.25 = bf16[128,512]{1,0:T(8,128)(2,1)S(1)} collective-permute-done((bf16[128,512]{1,0:T(8,128)(2,1)S(1)}, bf16[128,512]{1,0:T(8,128)(2,1)S(1)}, u32[]{:S(2)}, u32[]{:S(2)}) %collective-permute-start.25) | collective-permute-done | bytes 131104 | tf_op jit(solution)/shard_map/ppermute | solution.py:242
  64.4 1.3 %collective-permute-start.12 = (bf16[128,1280]{1,0:T(8,128)(2,1)S(1)}, bf16[128,1280]{1,0:T(8,128)(2,1)S(1)}, u32[]{:S(2)}, u32[]{:S(2)}) collective-permute-start(bf16[128,1280]{1,0:T(8,128)(2,1)S(1)} %get-tuple-element.23), channel_id=1, source_target_pairs={{8,0},{16,8},{24,16},{9,1},{17,9},{25,17},{10,2},{18,10},{26,18},{... | collective-permute-start | bytes 983048 | tf_op jit(solution)/shard_map/ppermute | solution.py:292
  65.7 1.3 %collective-permute-start.13 = (bf16[128,1280]{1,0:T(8,128)(2,1)S(1)}, bf16[128,1280]{1,0:T(8,128)(2,1)S(1)}, u32[]{:S(2)}, u32[]{:S(2)}) collective-permute-start(bf16[128,1280]{1,0:T(8,128)(2,1)S(1)} %get-tuple-element.24), channel_id=1, source_target_pairs={{8,0},{16,8},{24,16},{9,1},{17,9},{25,17},{10,2},{18,10},{26,18},{... | collective-permute-start | bytes 983048 | tf_op jit(solution)/shard_map/ppermute | solution.py:292
  67.0 3.2 %collective-permute-done.23 = bf16[128,512]{1,0:T(8,128)(2,1)S(1)} collective-permute-done((bf16[128,512]{1,0:T(8,128)(2,1)S(1)}, bf16[128,512]{1,0:T(8,128)(2,1)S(1)}, u32[]{:S(2)}, u32[]{:S(2)}) %collective-permute-start.23) | collective-permute-done | bytes 131104 | tf_op jit(solution)/shard_map/ppermute | solution.py:242
  70.2 0.9 collective-permute-start.19
  71.1 5.7 %collective-permute-done.26 = bf16[128,512]{1,0:T(8,128)(2,1)S(1)} collective-permute-done((bf16[128,512]{1,0:T(8,128)(2,1)S(1)}, bf16[128,512]{1,0:T(8,128)(2,1)S(1)}, u32[]{:S(2)}, u32[]{:S(2)}) %collective-permute-start.26) | collective-permute-done | bytes 131104 | tf_op jit(solution)/shard_map/ppermute | solution.py:242
  76.8 0.8 collective-permute-start.9
  77.7 1.3 %collective-permute-done.19.refs_14_ = bf16[128,512]{1,0:T(8,128)(2,1)S(1)} collective-permute-done((bf16[128,512]{1,0:T(8,128)(2,1)S(1)}, bf16[128,512]{1,0:T(8,128)(2,1)S(1)}, u32[]{:S(2)}, u32[]{:S(2)}) %collective-permute-start.19) | collective-permute-done | bytes 131104 | tf_op jit(solution)/shard_map/ppermute | solution.py:242
  79.0 0.9 collective-permute-start.24
  79.9 3.2 %collective-permute-done.20.refs_15_ = bf16[128,512]{1,0:T(8,128)(2,1)S(1)} collective-permute-done((bf16[128,512]{1,0:T(8,128)(2,1)S(1)}, bf16[128,512]{1,0:T(8,128)(2,1)S(1)}, u32[]{:S(2)}, u32[]{:S(2)}) %collective-permute-start.20) | collective-permute-done | bytes 131104 | tf_op jit(solution)/shard_map/ppermute | solution.py:242
  83.1 14.6 %shard_map.95 = (bf16[128,1280]{1,0:T(8,128)(2,1)S(1)}, bf16[128,1280]{1,0:T(8,128)(2,1)S(1)}, bf16[128,512]{1,0:T(8,128)(2,1)S(1)}, bf16[128,512]{1,0:T(8,128)(...) custom-call(s32[2,1,8,8]{3,2,1,0:T(8,128)S(1)} %copy-done, ...), custom_call_target="tpu_custom_call" | custom-call | flops 4000000000 | bytes 4000000 | tf_op jit(solution)/shard_map/pallas_call | solution.py:204
  97.7 0.1 collective-permute-start.29
  97.7 0.2 collective-permute-start.32
  97.9 2.1 %collective-permute-start.21 = (bf16[128,1280]{1,0:T(8,128)(2,1)S(1)}, bf16[128,1280]{1,0:T(8,128)(2,1)S(1)}, u32[]{:S(2)}, u32[]{:S(2)}) collective-permute-start(bf16[128,1280]{1,0:T(8,128)(2,1)S(1)} %get-tuple-element.26), channel_id=1, source_target_pairs={{0,1},{1,0},{2,3},{3,2},{4,5},{5,4},{6,7},{7,6},{8,9},{9,8},{10,11... | collective-permute-start | bytes 983048 | tf_op jit(solution)/shard_map/ppermute | solution.py:239
  100.1 1.0 maximum_select_fusion
  101.1 0.1 collective-permute-start.28
  101.3 2.3 %collective-permute-done.29 = bf16[128,512]{1,0:T(8,128)(2,1)S(1)} collective-permute-done((bf16[128,512]{1,0:T(8,128)(2,1)S(1)}, bf16[128,512]{1,0:T(8,128)(2,1)S(1)}, u32[]{:S(2)}, u32[]{:S(2)}) %collective-permute-start.29) | collective-permute-done | bytes 131104 | tf_op jit(solution)/shard_map/ppermute | solution.py:242
  103.6 0.1 collective-permute-start.30
  103.7 1.3 %collective-permute-done.32 = bf16[128,512]{1,0:T(8,128)(2,1)S(1)} collective-permute-done((bf16[128,512]{1,0:T(8,128)(2,1)S(1)}, bf16[128,512]{1,0:T(8,128)(2,1)S(1)}, u32[]{:S(2)}, u32[]{:S(2)}) %collective-permute-start.32) | collective-permute-done | bytes 131104 | tf_op jit(solution)/shard_map/ppermute | solution.py:242
  105.0 1.0 collective-permute-start.33
  106.1 2.9 %collective-permute-done.28 = bf16[128,512]{1,0:T(8,128)(2,1)S(1)} collective-permute-done((bf16[128,512]{1,0:T(8,128)(2,1)S(1)}, bf16[128,512]{1,0:T(8,128)(2,1)S(1)}, u32[]{:S(2)}, u32[]{:S(2)}) %collective-permute-start.28) | collective-permute-done | bytes 131104 | tf_op jit(solution)/shard_map/ppermute | solution.py:239
  109.1 1.1 collective-permute-done.30
  110.3 0.1 collective-permute-start.31
  110.4 2.7 %collective-permute-done.33 = bf16[128,512]{1,0:T(8,128)(2,1)S(1)} collective-permute-done((bf16[128,512]{1,0:T(8,128)(2,1)S(1)}, bf16[128,512]{1,0:T(8,128)(2,1)S(1)}, u32[]{:S(2)}, u32[]{:S(2)}) %collective-permute-start.33) | collective-permute-done | bytes 131104 | tf_op jit(solution)/shard_map/ppermute | solution.py:242
  113.1 0.1 collective-permute-start.34
  113.2 1.0 maximum_select_fusion.1
  114.2 6.3 %collective-permute-done.34 = bf16[128,512]{1,0:T(8,128)(2,1)S(1)} collective-permute-done((bf16[128,512]{1,0:T(8,128)(2,1)S(1)}, bf16[128,512]{1,0:T(8,128)(2,1)S(1)}, u32[]{:S(2)}, u32[]{:S(2)}) %collective-permute-start.34) | collective-permute-done | bytes 131104 | tf_op jit(solution)/shard_map/ppermute | solution.py:242
  120.5 1.6 %collective-permute-start.35 = (bf16[128,512]{1,0:T(8,128)(2,1)S(1)}, bf16[128,512]{1,0:T(8,128)(2,1)S(1)}, u32[]{:S(2)}, u32[]{:S(2)}) collective-permute-start(bf16[128,512]{1,0:T(8,128)(2,1)S(1)} %add_convert_fusion), channel_id=1, source_target_pairs={{0,1},{1,0},{2,3},{3,2},{4,5},{5,4},{6,7},{7,6},{8,9},{9,8},{10,11... | collective-permute-start | bytes 393224 | tf_op jit(solution)/shard_map/ppermute | solution.py:239
  122.1 3.8 %collective-permute-done.35 = bf16[128,512]{1,0:T(8,128)(2,1)S(1)} collective-permute-done((bf16[128,512]{1,0:T(8,128)(2,1)S(1)}, bf16[128,512]{1,0:T(8,128)(2,1)S(1)}, u32[]{:S(2)}, u32[]{:S(2)}) %collective-permute-start.35) | collective-permute-done | bytes 131104 | tf_op jit(solution)/shard_map/ppermute | solution.py:239
  126.1 0.8 maximum_bitcast_fusion
  (56 shorter events, 0.8 us)
Async XLA Ops:
  2.7 6.5 %collective-permute-start.2 = (bf16[128,512]{1,0:T(8,128)(2,1)S(1)}, bf16[128,512]{1,0:T(8,128)(2,1)S(1)}, u32[]{:S(2)}, u32[]{:S(2)}) collective-permute-start(bf16[128,512]{1,0:T(8,128)(2,1)S(1)} %pad_maximum_fusion.1), channel_id=1, source_target_pairs={{0,1},{1,0},{2,3},{3,2},{4,5},{5,4},{6,7},{7,6},{8,9},{9,8},{10,11... | collective-permute-start | bytes 393224 | tf_op jit(solution)/shard_map/ppermute | solution.py:239
  5.8 6.9 %collective-permute-start.3 = (bf16[128,512]{1,0:T(8,128)(2,1)S(1)}, bf16[128,512]{1,0:T(8,128)(2,1)S(1)}, u32[]{:S(2)}, u32[]{:S(2)}) collective-permute-start(bf16[128,512]{1,0:T(8,128)(2,1)S(1)} %pad_maximum_fusion.refs_6_), channel_id=1, source_target_pairs={{0,2},{1,3},{2,6},{3,7},{6,4},{7,5},{4,0},{5,1},{8,10},{9,11},{10,... | collective-permute-start | bytes 393224 | tf_op jit(solution)/shard_map/ppermute | solution.py:242
  8.8 8.4 %copy-start.2 = (bf16[1,128,2560]{2,1,0:T(8,128)(2,1)S(1)}, bf16[1,128,2560]{2,1,0:T(8,128)(2,1)}, u32[]{:S(2)}) copy-start(bf16[1,128,2560]{2,1,0:T(8,128)(2,1)} %param.10) | copy-start | bytes 1966084
  9.2 6.4 %collective-permute-start.4 = (bf16[128,512]{1,0:T(8,128)(2,1)S(1)}, bf16[128,512]{1,0:T(8,128)(2,1)S(1)}, u32[]{:S(2)}, u32[]{:S(2)}) collective-permute-start(bf16[128,512]{1,0:T(8,128)(2,1)S(1)} %collective-permute-done.2.refs_7_), channel_id=1, source_target_pairs={{0,2},{1,3},{2,6},{3,7},{6,4},{7,5},{4,0},{5,1},{8,10},{9,11},{10,... | collective-permute-start | bytes 393224 | tf_op jit(solution)/shard_map/ppermute | solution.py:242
  11.5 22.4 %copy-start = (s32[2,1,8,8]{3,2,1,0:T(8,128)S(1)}, s32[2,1,8,8]{3,2,1,0:T(8,128)}, u32[]{:S(2)}) copy-start(s32[2,1,8,8]{3,2,1,0:T(8,128)} %refs_0_.3) | copy-start | bytes 1540
  11.5 22.4 %copy-start.1 = (s32[2,1,8]{2,1,0:T(1,128)S(1)}, s32[2,1,8]{2,1,0:T(1,128)}, u32[]{:S(2)}) copy-start(s32[2,1,8]{2,1,0:T(1,128)} %refs_1_.3) | copy-start | bytes 196
  11.5 20.4 %collective-permute-start = (bf16[128,1280]{1,0:T(8,128)(2,1)S(1)}, bf16[128,1280]{1,0:T(8,128)(2,1)S(1)}, u32[]{:S(2)}, u32[]{:S(2)}) collective-permute-start(bf16[128,1280]{1,0:T(8,128)(2,1)S(1)} %get-tuple-element.54), channel_id=1, source_target_pairs={{0,1},{1,0},{2,3},{3,2},{4,5},{5,4},{6,7},{7,6},{8,9},{9,8},{10,11... | collective-permute-start | bytes 983048 | tf_op jit(solution)/shard_map/ppermute | solution.py:239
  12.7 7.0 %collective-permute-start.5 = (bf16[128,512]{1,0:T(8,128)(2,1)S(1)}, bf16[128,512]{1,0:T(8,128)(2,1)S(1)}, u32[]{:S(2)}, u32[]{:S(2)}) collective-permute-start(bf16[128,512]{1,0:T(8,128)(2,1)S(1)} %collective-permute-done.3.refs_8_), channel_id=1, source_target_pairs={{0,2},{1,3},{2,6},{3,7},{6,4},{7,5},{4,0},{5,1},{8,10},{9,11},{10,... | collective-permute-start | bytes 393224 | tf_op jit(solution)/shard_map/ppermute | solution.py:242
  15.6 7.1 %collective-permute-start.6 = (bf16[128,512]{1,0:T(8,128)(2,1)S(1)}, bf16[128,512]{1,0:T(8,128)(2,1)S(1)}, u32[]{:S(2)}, u32[]{:S(2)}) collective-permute-start(bf16[128,512]{1,0:T(8,128)(2,1)S(1)} %collective-permute-done.4.refs_9_), channel_id=1, source_target_pairs={{0,2},{1,3},{2,6},{3,7},{6,4},{7,5},{4,0},{5,1},{8,10},{9,11},{10,... | collective-permute-start | bytes 393224 | tf_op jit(solution)/shard_map/ppermute | solution.py:242
  17.2 16.2 %collective-permute-start.1 = (bf16[128,1280]{1,0:T(8,128)(2,1)S(1)}, bf16[128,1280]{1,0:T(8,128)(2,1)S(1)}, u32[]{:S(2)}, u32[]{:S(2)}) collective-permute-start(bf16[128,1280]{1,0:T(8,128)(2,1)S(1)} %get-tuple-element.52), channel_id=1, source_target_pairs={{0,1},{1,0},{2,3},{3,2},{4,5},{5,4},{6,7},{7,6},{8,9},{9,8},{10,11... | collective-permute-start | bytes 983048 | tf_op jit(solution)/shard_map/ppermute | solution.py:239
  18.6 11.4 %collective-permute-start.14 = (bf16[128,512]{1,0:T(8,128)(2,1)S(1)}, bf16[128,512]{1,0:T(8,128)(2,1)S(1)}, u32[]{:S(2)}, u32[]{:S(2)}) collective-permute-start(bf16[128,512]{1,0:T(8,128)(2,1)S(1)} %pad_maximum_fusion.3), channel_id=1, source_target_pairs={{0,1},{1,0},{2,3},{3,2},{4,5},{5,4},{6,7},{7,6},{8,9},{9,8},{10,11... | collective-permute-start | bytes 393224 | tf_op jit(solution)/shard_map/ppermute | solution.py:239
  19.7 14.2 %collective-permute-start.7 = (bf16[128,512]{1,0:T(8,128)(2,1)S(1)}, bf16[128,512]{1,0:T(8,128)(2,1)S(1)}, u32[]{:S(2)}, u32[]{:S(2)}) collective-permute-start(bf16[128,512]{1,0:T(8,128)(2,1)S(1)} %collective-permute-done.5.refs_10_), channel_id=1, source_target_pairs={{0,2},{1,3},{2,6},{3,7},{6,4},{7,5},{4,0},{5,1},{8,10},{9,11},{10,... | collective-permute-start | bytes 393224 | tf_op jit(solution)/shard_map/ppermute | solution.py:242
  22.8 11.1 %collective-permute-start.8 = (bf16[128,512]{1,0:T(8,128)(2,1)S(1)}, bf16[128,512]{1,0:T(8,128)(2,1)S(1)}, u32[]{:S(2)}, u32[]{:S(2)}) collective-permute-start(bf16[128,512]{1,0:T(8,128)(2,1)S(1)} %collective-permute-done.6.refs_11_), channel_id=1, source_target_pairs={{0,2},{1,3},{2,6},{3,7},{6,4},{7,5},{4,0},{5,1},{8,10},{9,11},{10,... | collective-permute-start | bytes 393224 | tf_op jit(solution)/shard_map/ppermute | solution.py:242
  30.0 22.3 %collective-permute-start.15 = (bf16[128,512]{1,0:T(8,128)(2,1)S(1)}, bf16[128,512]{1,0:T(8,128)(2,1)S(1)}, u32[]{:S(2)}, u32[]{:S(2)}) collective-permute-start(bf16[128,512]{1,0:T(8,128)(2,1)S(1)} %pad_maximum_fusion.2.refs_8_), channel_id=1, source_target_pairs={{0,2},{1,3},{2,6},{3,7},{6,4},{7,5},{4,0},{5,1},{8,10},{9,11},{10,... | collective-permute-start | bytes 393224 | tf_op jit(solution)/shard_map/ppermute | solution.py:242
  31.9 33.7 %collective-permute-start.10 = (bf16[128,1280]{1,0:T(8,128)(2,1)}, bf16[128,1280]{1,0:T(8,128)(2,1)S(1)}, u32[]{:S(2)}, u32[]{:S(2)}) collective-permute-start(bf16[128,1280]{1,0:T(8,128)(2,1)} %get-tuple-element.50), channel_id=1, source_target_pairs={{0,1},{1,0},{2,3},{3,2},{4,5},{5,4},{6,7},{7,6},{8,9},{9,8},{10,11... | collective-permute-start | bytes 983048 | tf_op jit(solution)/shard_map/ppermute | solution.py:239
  33.4 18.9 %collective-permute-start.16 = (bf16[128,512]{1,0:T(8,128)(2,1)S(1)}, bf16[128,512]{1,0:T(8,128)(2,1)S(1)}, u32[]{:S(2)}, u32[]{:S(2)}) collective-permute-start(bf16[128,512]{1,0:T(8,128)(2,1)S(1)} %collective-permute-done.14.refs_9_), channel_id=1, source_target_pairs={{0,2},{1,3},{2,6},{3,7},{6,4},{7,5},{4,0},{5,1},{8,10},{9,11},{10,... | collective-permute-start | bytes 393224 | tf_op jit(solution)/shard_map/ppermute | solution.py:242
  33.9 17.1 %copy-start.3 = (bf16[1,128,2560]{2,1,0:T(8,128)(2,1)S(1)}, bf16[1,128,2560]{2,1,0:T(8,128)(2,1)}, u32[]{:S(2)}) copy-start(bf16[1,128,2560]{2,1,0:T(8,128)(2,1)} %param.11) | copy-start | bytes 1966084
  50.9 7.5 %collective-permute-start.22 = (bf16[128,512]{1,0:T(8,128)(2,1)S(1)}, bf16[128,512]{1,0:T(8,128)(2,1)}, u32[]{:S(2)}, u32[]{:S(2)}) collective-permute-start(bf16[128,512]{1,0:T(8,128)(2,1)S(1)} %get-tuple-element.27), channel_id=1, source_target_pairs={{0,2},{1,3},{2,6},{3,7},{6,4},{7,5},{4,0},{5,1},{8,10},{9,11},{10,... | collective-permute-start | bytes 393224 | tf_op jit(solution)/shard_map/ppermute | solution.py:242
  51.8 25.0 %collective-permute-start.11 = (bf16[128,1280]{1,0:T(8,128)(2,1)}, bf16[128,1280]{1,0:T(8,128)(2,1)S(1)}, u32[]{:S(2)}, u32[]{:S(2)}) collective-permute-start(bf16[128,1280]{1,0:T(8,128)(2,1)} %get-tuple-element.48), channel_id=1, source_target_pairs={{0,1},{1,0},{2,3},{3,2},{4,5},{5,4},{6,7},{7,6},{8,9},{9,8},{10,11... | collective-permute-start | bytes 983048 | tf_op jit(solution)/shard_map/ppermute | solution.py:239
  52.3 12.1 %collective-permute-start.17 = (bf16[128,512]{1,0:T(8,128)(2,1)S(1)}, bf16[128,512]{1,0:T(8,128)(2,1)S(1)}, u32[]{:S(2)}, u32[]{:S(2)}) collective-permute-start(bf16[128,512]{1,0:T(8,128)(2,1)S(1)} %collective-permute-done.15.refs_10_), channel_id=1, source_target_pairs={{0,2},{1,3},{2,6},{3,7},{6,4},{7,5},{4,0},{5,1},{8,10},{9,11},{10,... | collective-permute-start | bytes 393224 | tf_op jit(solution)/shard_map/ppermute | solution.py:242
  52.3 17.9 %collective-permute-start.18 = (bf16[128,512]{1,0:T(8,128)(2,1)S(1)}, bf16[128,512]{1,0:T(8,128)(2,1)S(1)}, u32[]{:S(2)}, u32[]{:S(2)}) collective-permute-start(bf16[128,512]{1,0:T(8,128)(2,1)S(1)} %collective-permute-done.16.refs_11_), channel_id=1, source_target_pairs={{0,2},{1,3},{2,6},{3,7},{6,4},{7,5},{4,0},{5,1},{8,10},{9,11},{10,... | collective-permute-start | bytes 393224 | tf_op jit(solution)/shard_map/ppermute | solution.py:242
  58.4 5.9 %collective-permute-start.25 = (bf16[128,512]{1,0:T(8,128)(2,1)S(1)}, bf16[128,512]{1,0:T(8,128)(2,1)S(1)}, u32[]{:S(2)}, u32[]{:S(2)}) collective-permute-start(bf16[128,512]{1,0:T(8,128)(2,1)S(1)} %get-tuple-element.31), channel_id=1, source_target_pairs={{0,2},{1,3},{2,6},{3,7},{6,4},{7,5},{4,0},{5,1},{8,10},{9,11},{10,... | collective-permute-start | bytes 393224 | tf_op jit(solution)/shard_map/ppermute | solution.py:242
  64.3 5.9 %collective-permute-start.23 = (bf16[128,512]{1,0:T(8,128)(2,1)S(1)}, bf16[128,512]{1,0:T(8,128)(2,1)S(1)}, u32[]{:S(2)}, u32[]{:S(2)}) collective-permute-start(bf16[128,512]{1,0:T(8,128)(2,1)S(1)} %add_convert_fusion.11), channel_id=1, source_target_pairs={{0,2},{1,3},{2,6},{3,7},{6,4},{7,5},{4,0},{5,1},{8,10},{9,11},{10,... | collective-permute-start | bytes 393224 | tf_op jit(solution)/shard_map/ppermute | solution.py:242
  64.4 18.7 %collective-permute-start.12 = (bf16[128,1280]{1,0:T(8,128)(2,1)S(1)}, bf16[128,1280]{1,0:T(8,128)(2,1)S(1)}, u32[]{:S(2)}, u32[]{:S(2)}) collective-permute-start(bf16[128,1280]{1,0:T(8,128)(2,1)S(1)} %get-tuple-element.23), channel_id=1, source_target_pairs={{8,0},{16,8},{24,16},{9,1},{17,9},{25,17},{10,2},{18,10},{26,18},{... | collective-permute-start | bytes 983048 | tf_op jit(solution)/shard_map/ppermute | solution.py:292
  65.7 17.4 %collective-permute-start.13 = (bf16[128,1280]{1,0:T(8,128)(2,1)S(1)}, bf16[128,1280]{1,0:T(8,128)(2,1)S(1)}, u32[]{:S(2)}, u32[]{:S(2)}) collective-permute-start(bf16[128,1280]{1,0:T(8,128)(2,1)S(1)} %get-tuple-element.24), channel_id=1, source_target_pairs={{8,0},{16,8},{24,16},{9,1},{17,9},{25,17},{10,2},{18,10},{26,18},{... | collective-permute-start | bytes 983048 | tf_op jit(solution)/shard_map/ppermute | solution.py:292
  70.2 6.6 %collective-permute-start.26 = (bf16[128,512]{1,0:T(8,128)(2,1)S(1)}, bf16[128,512]{1,0:T(8,128)(2,1)S(1)}, u32[]{:S(2)}, u32[]{:S(2)}) collective-permute-start(bf16[128,512]{1,0:T(8,128)(2,1)S(1)} %add_convert_fusion.8), channel_id=1, source_target_pairs={{0,2},{1,3},{2,6},{3,7},{6,4},{7,5},{4,0},{5,1},{8,10},{9,11},{10,... | collective-permute-start | bytes 393224 | tf_op jit(solution)/shard_map/ppermute | solution.py:242
  70.2 8.8 %collective-permute-start.19 = (bf16[128,512]{1,0:T(8,128)(2,1)S(1)}, bf16[128,512]{1,0:T(8,128)(2,1)S(1)}, u32[]{:S(2)}, u32[]{:S(2)}) collective-permute-start(bf16[128,512]{1,0:T(8,128)(2,1)S(1)} %collective-permute-done.17.refs_12_), channel_id=1, source_target_pairs={{0,2},{1,3},{2,6},{3,7},{6,4},{7,5},{4,0},{5,1},{8,10},{9,11},{10,... | collective-permute-start | bytes 393224 | tf_op jit(solution)/shard_map/ppermute | solution.py:242
  76.8 6.3 %collective-permute-start.20 = (bf16[128,512]{1,0:T(8,128)(2,1)S(1)}, bf16[128,512]{1,0:T(8,128)(2,1)S(1)}, u32[]{:S(2)}, u32[]{:S(2)}) collective-permute-start(bf16[128,512]{1,0:T(8,128)(2,1)S(1)} %collective-permute-done.18.refs_13_), channel_id=1, source_target_pairs={{0,2},{1,3},{2,6},{3,7},{6,4},{7,5},{4,0},{5,1},{8,10},{9,11},{10,... | collective-permute-start | bytes 393224 | tf_op jit(solution)/shard_map/ppermute | solution.py:242
  76.8 21.1 %collective-permute-start.9 = (bf16[128,1280]{1,0:T(8,128)(2,1)S(1)}, bf16[128,1280]{1,0:T(8,128)(2,1)S(1)}, u32[]{:S(2)}, u32[]{:S(2)}) collective-permute-start(bf16[128,1280]{1,0:T(8,128)(2,1)S(1)} %get-tuple-element.24), channel_id=1, source_target_pairs={{0,1},{1,0},{2,3},{3,2},{4,5},{5,4},{6,7},{7,6},{8,9},{9,8},{10,11... | collective-permute-start | bytes 983048 | tf_op jit(solution)/shard_map/ppermute | solution.py:239
  79.0 22.2 %collective-permute-start.24 = (bf16[128,512]{1,0:T(8,128)(2,1)S(1)}, bf16[128,512]{1,0:T(8,128)(2,1)S(1)}, u32[]{:S(2)}, u32[]{:S(2)}) collective-permute-start(bf16[128,512]{1,0:T(8,128)(2,1)S(1)} %add_convert_fusion.10), channel_id=1, source_target_pairs={{0,2},{1,3},{2,6},{3,7},{6,4},{7,5},{4,0},{5,1},{8,10},{9,11},{10,... | collective-permute-start | bytes 393224 | tf_op jit(solution)/shard_map/ppermute | solution.py:242
  83.1 18.0 %collective-permute-start.27 = (bf16[128,512]{1,0:T(8,128)(2,1)S(1)}, bf16[128,512]{1,0:T(8,128)(2,1)S(1)}, u32[]{:S(2)}, u32[]{:S(2)}) collective-permute-start(bf16[128,512]{1,0:T(8,128)(2,1)S(1)} %add_convert_fusion.7), channel_id=1, source_target_pairs={{0,2},{1,3},{2,6},{3,7},{6,4},{7,5},{4,0},{5,1},{8,10},{9,11},{10,... | collective-permute-start | bytes 393224 | tf_op jit(solution)/shard_map/ppermute | solution.py:242
  97.7 5.9 %collective-permute-start.29 = (bf16[128,512]{1,0:T(8,128)(2,1)S(1)}, bf16[128,512]{1,0:T(8,128)(2,1)S(1)}, u32[]{:S(2)}, u32[]{:S(2)}) collective-permute-start(bf16[128,512]{1,0:T(8,128)(2,1)S(1)} %get-tuple-element.35), channel_id=1, source_target_pairs={{0,2},{1,3},{2,6},{3,7},{6,4},{7,5},{4,0},{5,1},{8,10},{9,11},{10,... | collective-permute-start | bytes 393224 | tf_op jit(solution)/shard_map/ppermute | solution.py:242
  97.7 7.3 %collective-permute-start.32 = (bf16[128,512]{1,0:T(8,128)(2,1)S(1)}, bf16[128,512]{1,0:T(8,128)(2,1)S(1)}, u32[]{:S(2)}, u32[]{:S(2)}) collective-permute-start(bf16[128,512]{1,0:T(8,128)(2,1)S(1)} %get-tuple-element.39), channel_id=1, source_target_pairs={{0,2},{1,3},{2,6},{3,7},{6,4},{7,5},{4,0},{5,1},{8,10},{9,11},{10,... | collective-permute-start | bytes 393224 | tf_op jit(solution)/shard_map/ppermute | solution.py:242
  97.9 15.2 %collective-permute-start.21 = (bf16[128,1280]{1,0:T(8,128)(2,1)S(1)}, bf16[128,1280]{1,0:T(8,128)(2,1)S(1)}, u32[]{:S(2)}, u32[]{:S(2)}) collective-permute-start(bf16[128,1280]{1,0:T(8,128)(2,1)S(1)} %get-tuple-element.26), channel_id=1, source_target_pairs={{0,1},{1,0},{2,3},{3,2},{4,5},{5,4},{6,7},{7,6},{8,9},{9,8},{10,11... | collective-permute-start | bytes 983048 | tf_op jit(solution)/shard_map/ppermute | solution.py:239
  101.1 7.9 %collective-permute-start.28 = (bf16[128,512]{1,0:T(8,128)(2,1)S(1)}, bf16[128,512]{1,0:T(8,128)(2,1)S(1)}, u32[]{:S(2)}, u32[]{:S(2)}) collective-permute-start(bf16[128,512]{1,0:T(8,128)(2,1)S(1)} %add_convert_fusion.6), channel_id=1, source_target_pairs={{0,1},{1,0},{2,3},{3,2},{4,5},{5,4},{6,7},{7,6},{8,9},{9,8},{10,11... | collective-permute-start | bytes 393224 | tf_op jit(solution)/shard_map/ppermute | solution.py:239
  103.6 6.6 %collective-permute-start.30 = (bf16[128,512]{1,0:T(8,128)(2,1)S(1)}, bf16[128,512]{1,0:T(8,128)(2,1)S(1)}, u32[]{:S(2)}, u32[]{:S(2)}) collective-permute-start(bf16[128,512]{1,0:T(8,128)(2,1)S(1)} %add_convert_fusion.5), channel_id=1, source_target_pairs={{0,2},{1,3},{2,6},{3,7},{6,4},{7,5},{4,0},{5,1},{8,10},{9,11},{10,... | collective-permute-start | bytes 393224 | tf_op jit(solution)/shard_map/ppermute | solution.py:242
  105.0 8.0 %collective-permute-start.33 = (bf16[128,512]{1,0:T(8,128)(2,1)S(1)}, bf16[128,512]{1,0:T(8,128)(2,1)S(1)}, u32[]{:S(2)}, u32[]{:S(2)}) collective-permute-start(bf16[128,512]{1,0:T(8,128)(2,1)S(1)} %add_convert_fusion.2), channel_id=1, source_target_pairs={{0,2},{1,3},{2,6},{3,7},{6,4},{7,5},{4,0},{5,1},{8,10},{9,11},{10,... | collective-permute-start | bytes 393224 | tf_op jit(solution)/shard_map/ppermute | solution.py:242
  110.3 11.8 %collective-permute-start.31 = (bf16[128,512]{1,0:T(8,128)(2,1)S(1)}, bf16[128,512]{1,0:T(8,128)(2,1)S(1)}, u32[]{:S(2)}, u32[]{:S(2)}) collective-permute-start(bf16[128,512]{1,0:T(8,128)(2,1)S(1)} %add_convert_fusion.4), channel_id=1, source_target_pairs={{0,2},{1,3},{2,6},{3,7},{6,4},{7,5},{4,0},{5,1},{8,10},{9,11},{10,... | collective-permute-start | bytes 393224 | tf_op jit(solution)/shard_map/ppermute | solution.py:242
  113.1 7.3 %collective-permute-start.34 = (bf16[128,512]{1,0:T(8,128)(2,1)S(1)}, bf16[128,512]{1,0:T(8,128)(2,1)S(1)}, u32[]{:S(2)}, u32[]{:S(2)}) collective-permute-start(bf16[128,512]{1,0:T(8,128)(2,1)S(1)} %add_convert_fusion.1), channel_id=1, source_target_pairs={{0,2},{1,3},{2,6},{3,7},{6,4},{7,5},{4,0},{5,1},{8,10},{9,11},{10,... | collective-permute-start | bytes 393224 | tf_op jit(solution)/shard_map/ppermute | solution.py:242
  120.5 5.5 %collective-permute-start.35 = (bf16[128,512]{1,0:T(8,128)(2,1)S(1)}, bf16[128,512]{1,0:T(8,128)(2,1)S(1)}, u32[]{:S(2)}, u32[]{:S(2)}) collective-permute-start(bf16[128,512]{1,0:T(8,128)(2,1)S(1)} %add_convert_fusion), channel_id=1, source_target_pairs={{0,1},{1,0},{2,3},{3,2},{4,5},{5,4},{6,7},{7,6},{8,9},{9,8},{10,11... | collective-permute-start | bytes 393224 | tf_op jit(solution)/shard_map/ppermute | solution.py:239

commit v2 on v1

v2 whole, which is shorter than its diff:
```python
import math

import jax
import jax.numpy as jnp
from jax import lax
from jax.experimental import pallas as pl
from jax.experimental.pallas import tpu as pltpu
from jax.sharding import PartitionSpec as P

QUERY_HEADS = 20
KEY_VALUE_HEADS = 4
HEAD_DIMENSION = 128
FILE_BLOCK_SIZE = 128
MICRO_BATCHES = 2

GROUP = QUERY_HEADS // KEY_VALUE_HEADS
SIDES = 2
HALF_KV = KEY_VALUE_HEADS // SIDES
HALF_Q_WIDTH = HALF_KV * GROUP * HEAD_DIMENSION
HALF_KV_WIDTH = HALF_KV * HEAD_DIMENSION
STACK = GROUP * FILE_BLOCK_SIZE
negative_large = -1e30
SCALE = 1.0 / math.sqrt(HEAD_DIMENSION)
EXP2_SCALE = SCALE * math.log2(math.e)

NT = (((1,), (1,)), ((), ()))
NN = (((1,), (0,)), ((), ()))
TN = (((0,), (0,)), ((), ()))


def folded_order(lines):
    return [0] + list(range(1, lines, 2)) + list(range(2, lines, 2))[::-1]


def line_position(line, lines):
    odd = lax.rem(line, 2) == 1
    return jnp.where(line == 0, 0, jnp.where(odd, (line + 1) // 2, lines - line // 2))


def position_line(position, lines):
    return jnp.where(
        position == 0, 0, jnp.where(position <= lines // 2, 2 * position - 1, 2 * (lines - position))
    )


def fold_rows(tile, op):
    rows, columns = tile.shape
    return op(tile.reshape(rows // 8, 8, columns), axis=0)


def backward_kernel(lines, micro, with_arrived, kv_count, *refs):
    tiles = lines * SIDES
    refs = list(refs)
    imports_ref, ids_ref, q_ref, g_ref, received_ref = refs[:5]
    at = 5
    arrived_ref = None
    if with_arrived:
        arrived_ref = refs[at]
        at += 1
    kv_refs = refs[at : at + kv_count]
    at += kv_count
    dq_ref = refs[at]
    at += 1
    dkv_refs = refs[at : at + lines]
    at += lines
    packed, q_stack, g_stack, scores, dprobs, dkv_sum, listing = refs[at:]

    me = lax.axis_index("ctx")
    line, side = me // SIDES, lax.rem(me, SIDES)
    position = line_position(line, lines)
    lane = side * HALF_Q_WIDTH

    def tile_value(tile):
        if kv_count == tiles:
            return kv_refs[tile][...]
        return kv_refs[tile // SIDES][tile % SIDES]

    evens, chunks = [], []
    for block in range(SIDES):
        query_slot = line * SIDES + (side if block == 0 else 1 - side)
        query_id = ids_ref[micro, 0, query_slot]
        others = []
        total = jnp.int32(1)
        for tile in range(tiles):
            if tile == block:
                continue
            step, chain = tile // SIDES, tile % SIDES
            key_line = position_line(lax.rem(position - step + lines, lines), lines)
            key_slot = key_line * SIDES + (side if chain == 0 else 1 - side)
            key_id = ids_ref[micro, 0, key_slot]
            live = imports_ref[micro, 0, query_id, key_id] > 0
            others.append((tile, live))
            total = total + jnp.where(live, 1, 0)
        even = lax.rem(total, 2) == 0
        evens.append(even)
        chunks.append((total + 1) // 2)
        listing[block, 0] = block
        listing[block, 1] = block
        packed[block, 0, :FILE_BLOCK_SIZE] = tile_value(block)
        packed[block, 0, FILE_BLOCK_SIZE:] = tile_value(block)
        place = jnp.where(even, 1, 2)
        for tile, live in others:

            def take(block=block, place=place, tile=tile):
                listing[block, place] = tile
                rows = pl.ds(
                    pl.multiple_of(lax.rem(place, 2) * FILE_BLOCK_SIZE, FILE_BLOCK_SIZE),
                    FILE_BLOCK_SIZE,
                )
                packed[block, place // 2, rows] = tile_value(tile)

            pl.when(live)(take)
            place = place + jnp.where(live, 1, 0)

    dkv_sum[...] = jnp.zeros_like(dkv_sum)

    triangle = lax.broadcasted_iota(jnp.int32, (FILE_BLOCK_SIZE, FILE_BLOCK_SIZE), 0) <= (
        lax.broadcasted_iota(jnp.int32, (FILE_BLOCK_SIZE, FILE_BLOCK_SIZE), 1)
    )
    allowed = jnp.concatenate([triangle] * GROUP, axis=1)
    head_columns = [
        slice(head * HEAD_DIMENSION, (head + 1) * HEAD_DIMENSION) for head in range(HALF_KV)
    ]
    value_columns = [
        slice(HALF_KV_WIDTH + head * HEAD_DIMENSION, HALF_KV_WIDTH + (head + 1) * HEAD_DIMENSION)
        for head in range(HALF_KV)
    ]

    for block in range(SIDES):
        for head in range(HALF_KV):
            for member in range(GROUP):
                rows = slice(member * FILE_BLOCK_SIZE, (member + 1) * FILE_BLOCK_SIZE)
                start = (head * GROUP + member) * HEAD_DIMENSION
                columns = slice(start, start + HEAD_DIMENSION)
                if block == 0:
                    wide = pl.ds(pl.multiple_of(lane + start, HEAD_DIMENSION), HEAD_DIMENSION)
                    q_stack[head, rows, :] = q_ref[micro, 0, :, wide]
                    upstream = g_ref[0, :, wide]
                else:
                    q_stack[head, rows, :] = received_ref[0, :, columns]
                    upstream = received_ref[1, :, columns]
                if with_arrived:
                    upstream = (
                        upstream.astype(jnp.float32)
                        + arrived_ref[block, :, columns].astype(jnp.float32)
                    ).astype(jnp.bfloat16)
                g_stack[head, rows, :] = upstream

        def products(chunk, head):
            score = lax.dot_general(
                packed[block, chunk, :, head_columns[head]],
                q_stack[head],
                NT,
                preferred_element_type=jnp.float32,
            )
            dprobs[head, chunk] = lax.dot_general(
                packed[block, chunk, :, value_columns[head]],
                g_stack[head],
                NT,
                preferred_element_type=jnp.float32,
            )
            return score

        def first(chunk, largest):
            found = []
            for head in range(HALF_KV):
                score = products(chunk, head)
                scores[head, chunk] = score
                found.append(jnp.maximum(largest[head], fold_rows(score, jnp.max)))
            return tuple(found)

        largest = []
        for head in range(HALF_KV):
            score = products(0, head)
            score = jnp.concatenate(
                [
                    jnp.where(allowed, score[:FILE_BLOCK_SIZE], negative_large),
                    score[FILE_BLOCK_SIZE:] + jnp.where(evens[block], 0.0, negative_large),
                ],
                axis=0,
            )
            scores[head, 0] = score
            largest.append(fold_rows(score, jnp.max))
        largest = lax.fori_loop(1, chunks[block], first, tuple(largest))
        row_max = [jnp.max(value, axis=0, keepdims=True) for value in largest]

        def second(chunk, sums):
            found = []
            for head in range(HALF_KV):
                weight = jnp.exp2((scores[head, chunk] - row_max[head]) * EXP2_SCALE)
                scores[head, chunk] = weight
                found.append(sums[2 * head] + fold_rows(weight, jnp.sum))
                found.append(sums[2 * head + 1] + fold_rows(weight * dprobs[head, chunk], jnp.sum))
            return tuple(found)

        nothing = jnp.zeros((8, STACK), jnp.float32)
        sums = lax.fori_loop(0, chunks[block], second, (nothing,) * (2 * HALF_KV))
        inverse = [1.0 / jnp.sum(sums[2 * h], axis=0, keepdims=True) for h in range(HALF_KV)]
        delta = [
            jnp.sum(sums[2 * h + 1], axis=0, keepdims=True) * inverse[h] for h in range(HALF_KV)
        ]

        def third(chunk, totals):
            found = []
            tile_pair = [listing[block, 2 * chunk], listing[block, 2 * chunk + 1]]
            for head in range(HALF_KV):
                prob = scores[head, chunk] * inverse[head]
                score_grad = (prob * (dprobs[head, chunk] - delta[head])).astype(jnp.bfloat16)
                key_part = lax.dot_general(
                    score_grad, q_stack[head], NN, preferred_element_type=jnp.float32
                )
                value_part = lax.dot_general(
                    prob.astype(jnp.bfloat16), g_stack[head], NN, preferred_element_type=jnp.float32
                )
                for place in range(2):
                    rows = slice(place * FILE_BLOCK_SIZE, (place + 1) * FILE_BLOCK_SIZE)
                    dkv_sum[tile_pair[place], :, head_columns[head]] += key_part[rows]
                    dkv_sum[tile_pair[place], :, value_columns[head]] += value_part[rows]
                found.append(
                    totals[head]
                    + lax.dot_general(
                        packed[block, chunk, :, head_columns[head]],
                        score_grad,
                        TN,
                        preferred_element_type=jnp.float32,
                    )
                )
            return tuple(found)

        empty = jnp.zeros((HEAD_DIMENSION, STACK), jnp.float32)
        dq_turned = lax.fori_loop(0, chunks[block], third, (empty,) * HALF_KV)
        for head in range(HALF_KV):
            for member in range(GROUP):
                start = (head * GROUP + member) * HEAD_DIMENSION
                part = dq_turned[head][:, member * FILE_BLOCK_SIZE : (member + 1) * FILE_BLOCK_SIZE]
                dq_ref[block, :, start : start + HEAD_DIMENSION] = (part.T * SCALE).astype(
                    jnp.bfloat16
                )

    for tile in range(tiles):
        out, chain = dkv_refs[tile // SIDES], tile % SIDES
        out[chain, :, :HALF_KV_WIDTH] = (dkv_sum[tile, :, :HALF_KV_WIDTH] * SCALE).astype(
            jnp.bfloat16
        )
        out[chain, :, HALF_KV_WIDTH:] = dkv_sum[tile, :, HALF_KV_WIDTH:].astype(jnp.bfloat16)


def backward(lines, micro, imports, block_ids, queries, gradient, received, arrived, kv_parts):
    tiles = lines * SIDES
    with_arrived = arrived is not None
    vmem = pl.BlockSpec(memory_space=pltpu.VMEM)
    smem = pl.BlockSpec(memory_space=pltpu.SMEM)
    operands = [imports, block_ids, queries, gradient, received]
    if with_arrived:
        operands.append(arrived)
    operands += kv_parts
    query_shape = (SIDES, FILE_BLOCK_SIZE, HALF_Q_WIDTH)
    key_shape = (SIDES, FILE_BLOCK_SIZE, 2 * HALF_KV_WIDTH)

    def body(*refs):
        backward_kernel(lines, micro, with_arrived, len(kv_parts), *refs)

    stacked = (HALF_KV, STACK, HEAD_DIMENSION)
    squares = (HALF_KV, tiles // 2, 2 * FILE_BLOCK_SIZE, STACK)
    results = pl.pallas_call(
        body,
        out_shape=[jax.ShapeDtypeStruct(query_shape, jnp.bfloat16)]
        + [jax.ShapeDtypeStruct(key_shape, jnp.bfloat16)] * lines,
        in_specs=[smem, smem] + [vmem] * (len(operands) - 2),
        out_specs=[vmem] * (1 + lines),
        scratch_shapes=[
            pltpu.VMEM((SIDES, tiles // 2, 2 * FILE_BLOCK_SIZE, 2 * HALF_KV_WIDTH), jnp.bfloat16),
            pltpu.VMEM(stacked, jnp.bfloat16),
            pltpu.VMEM(stacked, jnp.bfloat16),
            pltpu.VMEM(squares, jnp.float32),
            pltpu.VMEM(squares, jnp.float32),
            pltpu.VMEM((tiles, FILE_BLOCK_SIZE, 2 * HALF_KV_WIDTH), jnp.float32),
            pltpu.SMEM((SIDES, tiles), jnp.int32),
        ],
        compiler_params=pltpu.CompilerParams(vmem_limit_bytes=48 * 1024 * 1024),
        cost_estimate=pl.CostEstimate(
            flops=10 * 10**9, bytes_accessed=4 * 10**6, transcendentals=0
        ),
    )(*operands)
    return results[0], results[1:]


def on_device(queries, keys, values, grad_a, grad_b, imports, block_ids):
    devices = lax.axis_size("ctx")
    lines = devices // SIDES
    side = lax.rem(lax.axis_index("ctx"), SIDES)
    order = folded_order(lines)
    pairs = [(i, i ^ 1) for i in range(devices)]
    pipe = lax.axis_size("pipe")
    back = [(i + 1, i) for i in range(pipe - 1)]

    def swap(block):
        return lax.ppermute(block, "ctx", pairs)

    def turn(block, distance=1):
        route = [
            (order[i] * SIDES + s, order[(i + distance) % lines] * SIDES + s)
            for i in range(lines)
            for s in range(SIDES)
        ]
        return lax.ppermute(block, "ctx", route)

    def part(rows, width, of_side):
        return lax.dynamic_slice_in_dim(rows, of_side * width, width, 1)

    def key_part(micro, key_rows, value_rows, of_side):
        return jnp.concatenate(
            [
                part(key_rows[micro, 0], HALF_KV_WIDTH, of_side),
                part(value_rows[micro, 0], HALF_KV_WIDTH, of_side),
            ],
            axis=1,
        )

    def row_part(query_rows, gradient_rows):
        return jnp.stack(
            [
                part(query_rows, HALF_Q_WIDTH, 1 - side),
                part(gradient_rows, HALF_Q_WIDTH, 1 - side),
            ]
        )

    def joined(kept, received):
        ordered = jnp.concatenate([kept, received], axis=1)
        crossed = jnp.concatenate([received, kept], axis=1)
        return jnp.where(side == 0, ordered, crossed)

    def after(value, earlier):
        return lax.optimization_barrier((value, earlier))[0]

    def finished(sums):
        received = swap(sums[1])
        key_half = joined(sums[0][:, :HALF_KV_WIDTH], received[:, :HALF_KV_WIDTH])
        value_half = joined(sums[0][:, HALF_KV_WIDTH:], received[:, HALF_KV_WIDTH:])
        return jnp.concatenate([key_half, value_half], axis=1)

    def summed(parts, moved):
        total = parts[0].astype(jnp.float32)
        for block in moved:
            total = total + block.astype(jnp.float32)
        return total.astype(jnp.bfloat16)

    own = key_part(0, keys, values, side)
    given = key_part(0, keys, values, 1 - side)
    rows_a = swap(row_part(queries[0, 0], grad_a[0]))
    other = swap(given)
    tiles_a = [own, other]
    for _ in range(1, lines):
        own, other = turn(own), turn(other)
        tiles_a += [own, other]

    keys_b, values_b = lax.optimization_barrier((keys, values, tiles_a[1]))[:2]
    own_b = key_part(1, keys_b, values_b, side)
    other_b = swap(key_part(1, keys_b, values_b, 1 - side))
    unit_b = jnp.stack([own_b, other_b])
    unit_b = after(unit_b, tiles_a[2 * lines - 3]) if lines > 1 else unit_b
    queries_b, gradient_b = lax.optimization_barrier((queries, grad_b, tiles_a[3]))[:2]
    rows_b = swap(row_part(queries_b[1, 0], gradient_b[0]))
    units_b = [unit_b] + [turn(unit_b, step) for step in range(1, lines)]
    rows_a = after(rows_a, unit_b)

    dq_a, dkv_a = backward(
        lines, 0, imports, block_ids, queries, grad_a, rows_a, None, tiles_a
    )
    if lines > 1:
        dq_a, units_b[1] = lax.optimization_barrier((dq_a, units_b[1]))
    arrived = lax.ppermute(dq_a, "pipe", back)
    tied = lax.optimization_barrier((*units_b, *dkv_a))
    units_b, dkv_a = list(tied[:lines]), list(tied[lines:])
    back_a = swap(dq_a[1])
    moved_a = [turn(dkv_a[step], lines - step) for step in range(1, lines)]
    dq_b, dkv_b = backward(
        lines, 1, imports, block_ids, queries, grad_b, rows_b, arrived, units_b
    )
    moved_b = [turn(dkv_b[step], lines - step) for step in range(1, lines)]
    back_b = swap(dq_b[1])
    held = lax.optimization_barrier((moved_b[0], back_a, dkv_a[0], *moved_a))
    moved_b[0] = held[0]
    out_a = joined(dq_a[0], held[1])
    kv_a = finished(summed([held[2]], held[3:]))
    out_b = joined(dq_b[0], back_b)
    kv_b = finished(summed([dkv_b[0]], moved_b))
    kv = jnp.stack([kv_a, kv_b])
    return (out_a[None], out_b[None], kv[:, None])


def solution(mesh):
    return jax.shard_map(
        on_device,
        mesh=mesh,
        in_specs=(
            P(None, "pipe", "ctx", None),
            P(None, "pipe", "ctx", None),
            P(None, "pipe", "ctx", None),
            P("pipe", "ctx", None),
            P("pipe", "ctx", None),
            P(None, "pipe", None, None),
            P(None, "pipe", None),
        ),
        out_specs=(P("pipe", "ctx", None), P("pipe", "ctx", None), P(None, "pipe", "ctx", None)),
        check_vma=False,
    )
```

time: 125 us -> 110 us (0.88); the launches traced: 127 us -> 110 us
  Pallas kernels: 31.6 us -> 17.9 us
  waiting for transfers between devices: 48.8 us -> 43.5 us
  starting transfers between devices: 36 us -> 39 us
    pallas_call x2, Pallas kernels: 31.6 us -> 17.9 us  [backward(): pl.pallas_call(body, out_shape=[jax.ShapeDtypeStruct(query_shape, jnp.bfl...]
    ppermute x10 -> x8, waiting for transfers between devices: 13.2 us -> 5.13 us  [swap(): return lax.ppermute(block, 'ctx', pairs)]
    ppermute x26 -> x16, starting transfers between devices: 23 us -> 28.6 us  [the longest x15 27.3 us: turn(): return lax.ppermute(block, 'ctx', route)]
    ppermute x26 -> x16, waiting for transfers between devices: 35.7 us -> 38.4 us  [the longest x15 38.4 us: turn(): return lax.ppermute(block, 'ctx', route)]
    ppermute x10 -> x8, starting transfers between devices: 13 us -> 10.5 us  [swap(): return lax.ppermute(block, 'ctx', pairs)]
    unnamed x8 -> x28, local copies, waits for them, and re-layouts: 0.03 us -> 2.16 us
    dynamic_slice x6 -> x5, local copies, waits for them, and re-layouts: 1.69 us -> 0.1 us  [part(): return lax.dynamic_slice_in_dim(rows, of_side * width, width, 1)]
    slice x7 -> x16, local copies, waits for them, and re-layouts: 3.39 us -> 2.05 us  [the longest x3 0.99 us: key_part(): value_rows[micro, 0]]
  transfers between devices with their start and end apart: 36 -> 24, of which waited for: 17 -> 9; matrix products, arithmetic and copies ran while one was open for 5% -> 3% of each run, Pallas kernels for 25% -> 16%
where the time goes in v2:
time: 110 us
  waiting for transfers between devices  43.5 us (40%)
  starting transfers between devices  39 us (35%)
  Pallas kernels  17.9 us (16%)
  local copies, waits for them, and re-layouts  4.4 us (4%)
  other arithmetic  4.28 us (4%)
    ppermute x15, waiting for transfers between devices, turn(): return lax.ppermute(block, 'ctx', route)  38.4 us
    ppermute x15, starting transfers between devices, turn(): return lax.ppermute(block, 'ctx', route)  27.3 us
    pallas_call x2, Pallas kernels, backward(): pl.pallas_call(body, out_shape=[jax.ShapeDtypeStruct(query_shape, jnp.bfl...  17.9 us
    ppermute x8, starting transfers between devices, swap(): return lax.ppermute(block, 'ctx', pairs)  10.5 us
    ppermute x8, waiting for transfers between devices, swap(): return lax.ppermute(block, 'ctx', pairs)  5.13 us
  transfers between devices with their start and end apart: 24, of which 9 were waited for; matrix products, arithmetic and copies ran while one was open for 3% of the time, Pallas kernels for 16%

profile of v2, /device:TPU:0, one launch (start us, length us, event | category | flops | bytes accessed | tf_op | source)
XLA Modules:
  0.0 110.2 jit_solution(1098735590252104019)
XLA Ops:
  0.6 0.9 slice.73
  1.6 0.0 copy-start.1
  1.6 1.0 slice.74
  2.6 0.0 slice-start
  2.6 3.0 %collective-permute-start.1 = (bf16[128,512]{1,0:T(8,128)(2,1)S(1)}, bf16[128,512]{1,0:T(8,128)(2,1)S(1)}, u32[]{:S(2)}, u32[]{:S(2)}) collective-permute-start(bf16[128,512]{1,0:T(8,128)(2,1)S(1)} %pad_maximum_fusion.3), channel_id=1, source_target_pairs={{0,1},{1,0},{2,3},{3,2},{4,5},{5,4},{6,7},{7,6},{8,9},{9,8},{10,11... | collective-permute-start | bytes 393224 | tf_op jit(solution)/shard_map/ppermute | solution.py:298
  5.7 1.6 %collective-permute-start.5 = (bf16[128,512]{1,0:T(8,128)(2,1)S(1)}, bf16[128,512]{1,0:T(8,128)(2,1)S(1)}, u32[]{:S(2)}, u32[]{:S(2)}) collective-permute-start(bf16[128,512]{1,0:T(8,128)(2,1)S(1)} %pad_maximum_fusion.5.refs_5_), channel_id=1, source_target_pairs={{0,2},{1,3},{2,6},{3,7},{6,4},{7,5},{4,0},{5,1},{8,10},{9,11},{10,... | collective-permute-start | bytes 393224 | tf_op jit(solution)/shard_map/ppermute | solution.py:306
  7.3 0.0 slice-start.2
  7.4 0.0 copy-start.2
  7.4 0.1 pad_maximum_fusion
  7.5 0.6 collective-permute-start
  8.1 1.4 %collective-permute-done.1.refs_6_ = bf16[128,512]{1,0:T(8,128)(2,1)S(1)} collective-permute-done((bf16[128,512]{1,0:T(8,128)(2,1)S(1)}, bf16[128,512]{1,0:T(8,128)(2,1)S(1)}, u32[]{:S(2)}, u32[]{:S(2)}) %collective-permute-start.1) | collective-permute-done | bytes 131104 | tf_op jit(solution)/shard_map/ppermute | solution.py:298
  9.5 0.0 slice-start.1
  9.5 1.6 %collective-permute-start.3 = (bf16[128,512]{1,0:T(8,128)(2,1)S(1)}, bf16[128,512]{1,0:T(8,128)(2,1)S(1)}, u32[]{:S(2)}, u32[]{:S(2)}) collective-permute-start(bf16[128,512]{1,0:T(8,128)(2,1)S(1)} %collective-permute-done.1.refs_6_), channel_id=1, source_target_pairs={{0,2},{1,3},{2,6},{3,7},{6,4},{7,5},{4,0},{5,1},{8,10},{9,11},{10,... | collective-permute-start | bytes 393224 | tf_op jit(solution)/shard_map/ppermute | solution.py:306
  11.1 1.6 %collective-permute-start.2 = (bf16[128,512]{1,0:T(8,128)(2,1)S(1)}, bf16[128,512]{1,0:T(8,128)(2,1)S(1)}, u32[]{:S(2)}, u32[]{:S(2)}) collective-permute-start(bf16[128,512]{1,0:T(8,128)(2,1)S(1)} %pad_maximum_fusion.4), channel_id=1, source_target_pairs={{0,1},{1,0},{2,3},{3,2},{4,5},{5,4},{6,7},{7,6},{8,9},{9,8},{10,11... | collective-permute-start | bytes 393224 | tf_op jit(solution)/shard_map/ppermute | solution.py:298
  12.7 3.7 %collective-permute-start.6 = (bf16[128,512]{1,0:T(8,128)(2,1)S(1)}, bf16[128,512]{1,0:T(8,128)(2,1)S(1)}, u32[]{:S(2)}, u32[]{:S(2)}) collective-permute-start(bf16[128,512]{1,0:T(8,128)(2,1)S(1)} %collective-permute-done.5.refs_7_), channel_id=1, source_target_pairs={{0,2},{1,3},{2,6},{3,7},{6,4},{7,5},{4,0},{5,1},{8,10},{9,11},{10,... | collective-permute-start | bytes 393224 | tf_op jit(solution)/shard_map/ppermute | solution.py:306
  16.4 1.2 %collective-permute-done.3.refs_8_ = bf16[128,512]{1,0:T(8,128)(2,1)S(1)} collective-permute-done((bf16[128,512]{1,0:T(8,128)(2,1)S(1)}, bf16[128,512]{1,0:T(8,128)(2,1)S(1)}, u32[]{:S(2)}, u32[]{:S(2)}) %collective-permute-start.3) | collective-permute-done | bytes 131104 | tf_op jit(solution)/shard_map/ppermute | solution.py:306
  17.6 0.0 copy-start
  17.6 0.0 copy-start.9
  17.6 0.0 copy-start.12
  17.7 0.0 copy-start.13
  17.7 0.1 collective-permute-start.4
  17.7 2.5 %collective-permute-done.6.refs_9_ = bf16[128,512]{1,0:T(8,128)(2,1)S(1)} collective-permute-done((bf16[128,512]{1,0:T(8,128)(2,1)S(1)}, bf16[128,512]{1,0:T(8,128)(2,1)S(1)}, u32[]{:S(2)}, u32[]{:S(2)}) %collective-permute-start.6) | collective-permute-done | bytes 131104 | tf_op jit(solution)/shard_map/ppermute | solution.py:306
  20.2 2.3 %collective-permute-start.7 = (bf16[128,512]{1,0:T(8,128)(2,1)S(1)}, bf16[128,512]{1,0:T(8,128)(2,1)S(1)}, u32[]{:S(2)}, u32[]{:S(2)}) collective-permute-start(bf16[128,512]{1,0:T(8,128)(2,1)S(1)} %collective-permute-done.6.refs_9_), channel_id=1, source_target_pairs={{0,2},{1,3},{2,6},{3,7},{6,4},{7,5},{4,0},{5,1},{8,10},{9,11},{10,... | collective-permute-start | bytes 393224 | tf_op jit(solution)/shard_map/ppermute | solution.py:306
  22.5 1.1 collective-permute-done.4.refs_10_
  23.6 1.7 %collective-permute-start.8 = (bf16[128,512]{1,0:T(8,128)(2,1)S(1)}, bf16[128,512]{1,0:T(8,128)(2,1)S(1)}, u32[]{:S(2)}, u32[]{:S(2)}) collective-permute-start(bf16[128,512]{1,0:T(8,128)(2,1)S(1)} %collective-permute-done.4.refs_10_), channel_id=1, source_target_pairs={{0,2},{1,3},{2,6},{3,7},{6,4},{7,5},{4,0},{5,1},{8,10},{9,11},{10,... | collective-permute-start | bytes 393224 | tf_op jit(solution)/shard_map/ppermute | solution.py:306
  25.3 0.9 pad_maximum_fusion.1
  26.2 0.0 collective-permute-start.10
  26.2 1.8 %collective-permute-done.2 = bf16[128,512]{1,0:T(8,128)(2,1)S(1)} collective-permute-done((bf16[128,512]{1,0:T(8,128)(2,1)S(1)}, bf16[128,512]{1,0:T(8,128)(2,1)S(1)}, u32[]{:S(2)}, u32[]{:S(2)}) %collective-permute-start.2) | collective-permute-done | bytes 131104 | tf_op jit(solution)/shard_map/ppermute | solution.py:298
  28.1 2.0 %collective-permute-start.13 = (bf16[2,128,512]{2,1,0:T(8,128)(2,1)S(1)}, bf16[2,128,512]{2,1,0:T(8,128)(2,1)}, u32[]{:S(2)}, u32[]{:S(2)}) collective-permute-start(bf16[2,128,512]{2,1,0:T(8,128)(2,1)S(1)} %pad_maximum_fusion.2.refs_6_), channel_id=1, source_target_pairs={{0,4},{1,5},{2,0},{3,1},{6,2},{7,3},{4,6},{5,7},{8,12},{9,13},{10,... | collective-permute-start | bytes 786440 | tf_op jit(solution)/shard_map/ppermute | solution.py:306
  30.0 0.0 collective-permute-done.refs_4_
  30.1 3.0 %collective-permute-start.12 = (bf16[2,128,512]{2,1,0:T(8,128)(2,1)S(1)}, bf16[2,128,512]{2,1,0:T(8,128)(2,1)}, u32[]{:S(2)}, u32[]{:S(2)}) collective-permute-start(bf16[2,128,512]{2,1,0:T(8,128)(2,1)S(1)} %pad_maximum_fusion.2.refs_6_), channel_id=1, source_target_pairs={{0,6},{1,7},{2,4},{3,5},{6,0},{7,1},{4,2},{5,3},{8,14},{9,15},{10,... | collective-permute-start | bytes 786440 | tf_op jit(solution)/shard_map/ppermute | solution.py:306
  33.1 9.2 %shard_map.94 = (bf16[2,128,1280]{2,1,0:T(8,128)(2,1)S(1)}, bf16[2,128,512]{2,1,0:T(8,128)(2,1)S(1)}, bf16[2,128,512]{2,1,0:T(8,128)(2,1)S(1)}, bf16[2,128,512]{2,1,0:T(8,128)(2,1)S(1)}, bf16[2,128,512]{2,1,0:T(8,128)(2,1)S(1)}) custom-call(s32[2,1,8,8]{3,2,1,0:T(8,128)S(1)} %copy-done.12, s32[2,1,8]{2,1,0:T(1,128)S(1)} %copy-done.13, ...), custom_call_target="tpu_custom_call" | custom-call | flops 10000000000 | bytes 4000000 | tf_op jit(solution)/shard_map/pallas_call | solution.py:265
  42.4 0.0 copy-start.4
  42.4 0.7 copy-done.4
  43.1 0.7 copy-done.5
  43.8 8.8 %collective-permute-done.9.refs_7_ = bf16[2,128,512]{2,1,0:T(8,128)(2,1)S(1)} collective-permute-done((bf16[2,128,512]{2,1,0:T(8,128)(2,1)S(1)}, bf16[2,128,512]{2,1,0:T(8,128)(2,1)S(1)}, u32[]{:S(2)}, u32[]{:S(2)}) %collective-permute-start.9) | collective-permute-done | bytes 262176 | tf_op jit(solution)/shard_map/ppermute | solution.py:306
  52.5 0.7 copy-done.6
  53.2 1.3 %collective-permute-start.11 = (bf16[2,128,1280]{2,1,0:T(8,128)(2,1)S(1)}, bf16[2,128,1280]{2,1,0:T(8,128)(2,1)}, u32[]{:S(2)}, u32[]{:S(2)}) collective-permute-start(bf16[2,128,1280]{2,1,0:T(8,128)(2,1)S(1)} %get-tuple-element.40), channel_id=1, source_target_pairs={{8,0},{16,8},{24,16},{9,1},{17,9},{25,17},{10,2},{18,10},{26,18},{... | collective-permute-start | bytes 1966088 | tf_op jit(solution)/shard_map/ppermute | solution.py:372
  54.5 0.0 copy-start.7
  54.6 0.0 collective-permute-done.13.refs_9_
  54.6 0.1 collective-permute-start.16
  54.6 2.3 %collective-permute-start.17 = (bf16[2,128,512]{2,1,0:T(8,128)(2,1)}, bf16[2,128,512]{2,1,0:T(8,128)(2,1)S(1)}, u32[]{:S(2)}, u32[]{:S(2)}) collective-permute-start(bf16[2,128,512]{2,1,0:T(8,128)(2,1)} %copy-done.4), channel_id=1, source_target_pairs={{0,6},{1,7},{2,4},{3,5},{6,0},{7,1},{4,2},{5,3},{8,14},{9,15},{10,... | collective-permute-start | bytes 786440 | tf_op jit(solution)/shard_map/ppermute | solution.py:306
  56.9 1.0 collective-permute-start.18
  58.0 1.6 %collective-permute-start.15 = (bf16[128,1280]{1,0:T(8,128)(2,1)S(1)}, bf16[128,1280]{1,0:T(8,128)(2,1)S(1)}, u32[]{:S(2)}, u32[]{:S(2)}) collective-permute-start(bf16[128,1280]{1,0:T(8,128)(2,1)S(1)} %get-tuple-element.73), channel_id=1, source_target_pairs={{0,1},{1,0},{2,3},{3,2},{4,5},{5,4},{6,7},{7,6},{8,9},{9,8},{10,11... | collective-permute-start | bytes 983048 | tf_op jit(solution)/shard_map/ppermute | solution.py:298
  59.6 0.0 collective-permute-done.11.refs_5_
  59.6 8.7 %shard_map.95 = (bf16[2,128,1280]{2,1,0:T(8,128)(2,1)S(1)}, bf16[2,128,512]{2,1,0:T(8,128)(2,1)S(1)}, bf16[2,128,512]{2,1,0:T(8,128)(2,1)S(1)}, bf16[2,128,512]{2,1,0:T(8,128)(2,1)S(1)}, bf16[2,128,512]{2,1,0:T(8,128)(2,1)S(1)}) custom-call(s32[2,1,8,8]{3,2,1,0:T(8,128)S(1)} %copy-done.12, s32[2,1,8]{2,1,0:T(1,128)S(1)} %copy-done.13, ...), custom_call_target="tpu_custom_call" | custom-call | flops 10000000000 | bytes 4000000 | tf_op jit(solution)/shard_map/pallas_call | solution.py:265
  68.3 0.4 collective-permute-start.14
  68.7 0.0 collective-permute-done.16
  68.7 2.9 %collective-permute-start.21 = (bf16[2,128,512]{2,1,0:T(8,128)(2,1)S(1)}, bf16[2,128,512]{2,1,0:T(8,128)(2,1)S(1)}, u32[]{:S(2)}, u32[]{:S(2)}) collective-permute-start(bf16[2,128,512]{2,1,0:T(8,128)(2,1)S(1)} %get-tuple-element.65), channel_id=1, source_target_pairs={{0,6},{1,7},{2,4},{3,5},{6,0},{7,1},{4,2},{5,3},{8,14},{9,15},{10,... | collective-permute-start | bytes 786440 | tf_op jit(solution)/shard_map/ppermute | solution.py:306
  71.6 4.7 %collective-permute-start.22 = (bf16[2,128,512]{2,1,0:T(8,128)(2,1)S(1)}, bf16[2,128,512]{2,1,0:T(8,128)(2,1)S(1)}, u32[]{:S(2)}, u32[]{:S(2)}) collective-permute-start(bf16[2,128,512]{2,1,0:T(8,128)(2,1)S(1)} %get-tuple-element.66), channel_id=1, source_target_pairs={{0,2},{1,3},{2,6},{3,7},{6,4},{7,5},{4,0},{5,1},{8,10},{9,11},{10,... | collective-permute-start | bytes 786440 | tf_op jit(solution)/shard_map/ppermute | solution.py:306
  76.3 16.0 %collective-permute-done.18 = bf16[2,128,512]{2,1,0:T(8,128)(2,1)S(1)} collective-permute-done((bf16[2,128,512]{2,1,0:T(8,128)(2,1)S(1)}, bf16[2,128,512]{2,1,0:T(8,128)(2,1)S(1)}, u32[]{:S(2)}, u32[]{:S(2)}) %collective-permute-start.18) | collective-permute-done | bytes 262176 | tf_op jit(solution)/shard_map/ppermute | solution.py:306
  92.3 1.5 %collective-permute-start.19 = (bf16[128,1280]{1,0:T(8,128)(2,1)S(1)}, bf16[128,1280]{1,0:T(8,128)(2,1)S(1)}, u32[]{:S(2)}, u32[]{:S(2)}) collective-permute-start(bf16[128,1280]{1,0:T(8,128)(2,1)S(1)} %get-tuple-element.71), channel_id=1, source_target_pairs={{0,1},{1,0},{2,3},{3,2},{4,5},{5,4},{6,7},{7,6},{8,9},{9,8},{10,11... | collective-permute-start | bytes 983048 | tf_op jit(solution)/shard_map/ppermute | solution.py:298
  93.8 0.0 collective-permute-done.15
  93.8 0.0 collective-permute-done.14
  93.8 0.1 add_convert_fusion.1
  94.0 0.6 collective-permute-start.20
  94.6 0.0 collective-permute-done.21
  94.6 8.9 %collective-permute-done.22 = bf16[2,128,512]{2,1,0:T(8,128)(2,1)S(1)} collective-permute-done((bf16[2,128,512]{2,1,0:T(8,128)(2,1)S(1)}, bf16[2,128,512]{2,1,0:T(8,128)(2,1)S(1)}, u32[]{:S(2)}, u32[]{:S(2)}) %collective-permute-start.22) | collective-permute-done | bytes 262176 | tf_op jit(solution)/shard_map/ppermute | solution.py:306
  103.5 0.1 add_convert_fusion
  103.7 1.6 %collective-permute-start.23 = (bf16[128,512]{1,0:T(8,128)(2,1)S(1)}, bf16[128,512]{1,0:T(8,128)(2,1)S(1)}, u32[]{:S(2)}, u32[]{:S(2)}) collective-permute-start(bf16[128,512]{1,0:T(8,128)(2,1)S(1)} %get-tuple-element.77), channel_id=1, source_target_pairs={{0,1},{1,0},{2,3},{3,2},{4,5},{5,4},{6,7},{7,6},{8,9},{9,8},{10,11... | collective-permute-start | bytes 393224 | tf_op jit(solution)/shard_map/ppermute | solution.py:298
  105.3 1.0 maximum_select_fusion
  106.3 1.0 maximum_select_fusion.1
  107.4 1.9 %collective-permute-done.23 = bf16[128,512]{1,0:T(8,128)(2,1)S(1)} collective-permute-done((bf16[128,512]{1,0:T(8,128)(2,1)S(1)}, bf16[128,512]{1,0:T(8,128)(2,1)S(1)}, u32[]{:S(2)}, u32[]{:S(2)}) %collective-permute-start.23) | collective-permute-done | bytes 131104 | tf_op jit(solution)/shard_map/ppermute | solution.py:298
  109.4 0.8 maximum_bitcast_fusion
  (57 shorter events, 0.6 us)
Async XLA Ops:
  1.6 5.7 %copy-start.1 = (bf16[1,128,2560]{2,1,0:T(8,128)(2,1)S(1)}, bf16[1,128,2560]{2,1,0:T(8,128)(2,1)}, u32[]{:S(2)}) copy-start(bf16[1,128,2560]{2,1,0:T(8,128)(2,1)} %refs_3_.2) | copy-start | bytes 1966084
  2.6 4.7 %slice-start = ((bf16[2,1,128,2560]{3,2,1,0:T(8,128)(2,1)}), bf16[1,1,128,2560]{3,2,1,0:T(8,128)(2,1)S(1)}, s32[]{:S(2)}) async-start(bf16[2,1,128,2560]{3,2,1,0:T(8,128)(2,1)} %refs_2_.3), calls=%async_computation | async-start | bytes 1310720 | tf_op jit(solution)/shard_map/slice | solution.py:350
  2.6 6.8 %collective-permute-start.1 = (bf16[128,512]{1,0:T(8,128)(2,1)S(1)}, bf16[128,512]{1,0:T(8,128)(2,1)S(1)}, u32[]{:S(2)}, u32[]{:S(2)}) collective-permute-start(bf16[128,512]{1,0:T(8,128)(2,1)S(1)} %pad_maximum_fusion.3), channel_id=1, source_target_pairs={{0,1},{1,0},{2,3},{3,2},{4,5},{5,4},{6,7},{7,6},{8,9},{9,8},{10,11... | collective-permute-start | bytes 393224 | tf_op jit(solution)/shard_map/ppermute | solution.py:298
  5.7 7.0 %collective-permute-start.5 = (bf16[128,512]{1,0:T(8,128)(2,1)S(1)}, bf16[128,512]{1,0:T(8,128)(2,1)S(1)}, u32[]{:S(2)}, u32[]{:S(2)}) collective-permute-start(bf16[128,512]{1,0:T(8,128)(2,1)S(1)} %pad_maximum_fusion.5.refs_5_), channel_id=1, source_target_pairs={{0,2},{1,3},{2,6},{3,7},{6,4},{7,5},{4,0},{5,1},{8,10},{9,11},{10,... | collective-permute-start | bytes 393224 | tf_op jit(solution)/shard_map/ppermute | solution.py:306
  7.3 2.1 %slice-start.3 = ((bf16[2,1,128,512]{3,2,1,0:T(8,128)(2,1)}), bf16[1,1,128,512]{3,2,1,0:T(8,128)(2,1)S(1)}, s32[]{:S(2)}) async-start(bf16[2,1,128,512]{3,2,1,0:T(8,128)(2,1)} %param.8), calls=%async_computation.3 | async-start | bytes 262144 | tf_op jit(solution)/shard_map/slice | solution.py:314
  7.3 2.1 %slice-start.2 = ((bf16[2,1,128,512]{3,2,1,0:T(8,128)(2,1)}), bf16[1,1,128,512]{3,2,1,0:T(8,128)(2,1)S(1)}, s32[]{:S(2)}) async-start(bf16[2,1,128,512]{3,2,1,0:T(8,128)(2,1)} %param.9), calls=%async_computation.2 | async-start | bytes 262144 | tf_op jit(solution)/shard_map/slice | solution.py:315
  7.4 10.2 %copy-start.2 = (bf16[1,128,2560]{2,1,0:T(8,128)(2,1)S(1)}, bf16[1,128,2560]{2,1,0:T(8,128)(2,1)}, u32[]{:S(2)}) copy-start(bf16[1,128,2560]{2,1,0:T(8,128)(2,1)} %refs_3_.3) | copy-start | bytes 1966084
  7.5 22.6 %collective-permute-start = (bf16[2,128,1280]{2,1,0:T(8,128)(2,1)S(1)}, bf16[2,128,1280]{2,1,0:T(8,128)(2,1)S(1)}, u32[]{:S(2)}, u32[]{:S(2)}) collective-permute-start(bf16[2,128,1280]{2,1,0:T(8,128)(2,1)S(1)} %pad_maximum_fusion), channel_id=1, source_target_pairs={{0,1},{1,0},{2,3},{3,2},{4,5},{5,4},{6,7},{7,6},{8,9},{9,8},{10,11... | collective-permute-start | bytes 1966088 | tf_op jit(solution)/shard_map/ppermute | solution.py:298
  9.4 8.2 %copy-start.8 = (bf16[128,512]{1,0:T(8,128)(2,1)}, bf16[128,512]{1,0:T(8,128)(2,1)S(1)}, u32[]{:S(2)}) copy-start(bf16[128,512]{1,0:T(8,128)(2,1)S(1)} %collective-permute-done.1.refs_6_) | copy-start | bytes 393220
  9.5 13.0 %slice-start.1 = ((bf16[2,1,128,2560]{3,2,1,0:T(8,128)(2,1)}), bf16[1,1,128,2560]{3,2,1,0:T(8,128)(2,1)S(1)}, s32[]{:S(2)}) async-start(bf16[2,1,128,2560]{3,2,1,0:T(8,128)(2,1)} %refs_2_.3), calls=%async_computation.1 | async-start | bytes 1310720 | tf_op jit(solution)/shard_map/slice | solution.py:363
  9.5 8.1 %collective-permute-start.3 = (bf16[128,512]{1,0:T(8,128)(2,1)S(1)}, bf16[128,512]{1,0:T(8,128)(2,1)S(1)}, u32[]{:S(2)}, u32[]{:S(2)}) collective-permute-start(bf16[128,512]{1,0:T(8,128)(2,1)S(1)} %collective-permute-done.1.refs_6_), channel_id=1, source_target_pairs={{0,2},{1,3},{2,6},{3,7},{6,4},{7,5},{4,0},{5,1},{8,10},{9,11},{10,... | collective-permute-start | bytes 393224 | tf_op jit(solution)/shard_map/ppermute | solution.py:306
  11.1 16.9 %collective-permute-start.2 = (bf16[128,512]{1,0:T(8,128)(2,1)S(1)}, bf16[128,512]{1,0:T(8,128)(2,1)S(1)}, u32[]{:S(2)}, u32[]{:S(2)}) collective-permute-start(bf16[128,512]{1,0:T(8,128)(2,1)S(1)} %pad_maximum_fusion.4), channel_id=1, source_target_pairs={{0,1},{1,0},{2,3},{3,2},{4,5},{5,4},{6,7},{7,6},{8,9},{9,8},{10,11... | collective-permute-start | bytes 393224 | tf_op jit(solution)/shard_map/ppermute | solution.py:298
  12.7 9.8 %copy-start.10 = (bf16[128,512]{1,0:T(8,128)(2,1)}, bf16[128,512]{1,0:T(8,128)(2,1)S(1)}, u32[]{:S(2)}) copy-start(bf16[128,512]{1,0:T(8,128)(2,1)S(1)} %collective-permute-done.5.refs_7_) | copy-start | bytes 393220
  12.7 7.5 %collective-permute-start.6 = (bf16[128,512]{1,0:T(8,128)(2,1)S(1)}, bf16[128,512]{1,0:T(8,128)(2,1)S(1)}, u32[]{:S(2)}, u32[]{:S(2)}) collective-permute-start(bf16[128,512]{1,0:T(8,128)(2,1)S(1)} %collective-permute-done.5.refs_7_), channel_id=1, source_target_pairs={{0,2},{1,3},{2,6},{3,7},{6,4},{7,5},{4,0},{5,1},{8,10},{9,11},{10,... | collective-permute-start | bytes 393224 | tf_op jit(solution)/shard_map/ppermute | solution.py:306
  17.6 15.5 %copy-start = (bf16[2,1,128,2560]{3,2,1,0:T(8,128)(2,1)S(1)}, bf16[2,1,128,2560]{3,2,1,0:T(8,128)(2,1)}, u32[]{:S(2)}) copy-start(bf16[2,1,128,2560]{3,2,1,0:T(8,128)(2,1)} %refs_2_.3) | copy-start | bytes 3932164
  17.6 15.4 %copy-start.9 = (bf16[128,512]{1,0:T(8,128)(2,1)S(1)}, bf16[128,512]{1,0:T(8,128)(2,1)}, u32[]{:S(2)}) copy-start(bf16[128,512]{1,0:T(8,128)(2,1)} %copy-done.8) | copy-start | bytes 393220
  17.6 15.4 %copy-start.12 = (s32[2,1,8,8]{3,2,1,0:T(8,128)S(1)}, s32[2,1,8,8]{3,2,1,0:T(8,128)}, u32[]{:S(2)}) copy-start(s32[2,1,8,8]{3,2,1,0:T(8,128)} %refs_0_.3) | copy-start | bytes 1540
  17.7 15.4 %copy-start.13 = (s32[2,1,8]{2,1,0:T(1,128)S(1)}, s32[2,1,8]{2,1,0:T(1,128)}, u32[]{:S(2)}) copy-start(s32[2,1,8]{2,1,0:T(1,128)} %refs_1_.3) | copy-start | bytes 196
  17.7 5.9 %collective-permute-start.4 = (bf16[128,512]{1,0:T(8,128)(2,1)S(1)}, bf16[128,512]{1,0:T(8,128)(2,1)S(1)}, u32[]{:S(2)}, u32[]{:S(2)}) collective-permute-start(bf16[128,512]{1,0:T(8,128)(2,1)S(1)} %collective-permute-done.3.refs_8_), channel_id=1, source_target_pairs={{0,2},{1,3},{2,6},{3,7},{6,4},{7,5},{4,0},{5,1},{8,10},{9,11},{10,... | collective-permute-start | bytes 393224 | tf_op jit(solution)/shard_map/ppermute | solution.py:306
  20.2 12.9 %collective-permute-start.7 = (bf16[128,512]{1,0:T(8,128)(2,1)S(1)}, bf16[128,512]{1,0:T(8,128)(2,1)S(1)}, u32[]{:S(2)}, u32[]{:S(2)}) collective-permute-start(bf16[128,512]{1,0:T(8,128)(2,1)S(1)} %collective-permute-done.6.refs_9_), channel_id=1, source_target_pairs={{0,2},{1,3},{2,6},{3,7},{6,4},{7,5},{4,0},{5,1},{8,10},{9,11},{10,... | collective-permute-start | bytes 393224 | tf_op jit(solution)/shard_map/ppermute | solution.py:306
  23.6 9.5 %copy-start.11 = (bf16[128,512]{1,0:T(8,128)(2,1)S(1)}, bf16[128,512]{1,0:T(8,128)(2,1)}, u32[]{:S(2)}) copy-start(bf16[128,512]{1,0:T(8,128)(2,1)} %copy-done.10) | copy-start | bytes 393220
  23.6 9.5 %collective-permute-start.8 = (bf16[128,512]{1,0:T(8,128)(2,1)S(1)}, bf16[128,512]{1,0:T(8,128)(2,1)S(1)}, u32[]{:S(2)}, u32[]{:S(2)}) collective-permute-start(bf16[128,512]{1,0:T(8,128)(2,1)S(1)} %collective-permute-done.4.refs_10_), channel_id=1, source_target_pairs={{0,2},{1,3},{2,6},{3,7},{6,4},{7,5},{4,0},{5,1},{8,10},{9,11},{10,... | collective-permute-start | bytes 393224 | tf_op jit(solution)/shard_map/ppermute | solution.py:306
  26.2 31.8 %collective-permute-start.10 = (bf16[2,128,1280]{2,1,0:T(8,128)(2,1)}, bf16[2,128,1280]{2,1,0:T(8,128)(2,1)}, u32[]{:S(2)}, u32[]{:S(2)}) collective-permute-start(bf16[2,128,1280]{2,1,0:T(8,128)(2,1)} %pad_maximum_fusion.1), channel_id=1, source_target_pairs={{0,1},{1,0},{2,3},{3,2},{4,5},{5,4},{6,7},{7,6},{8,9},{9,8},{10,11... | collective-permute-start | bytes 1966088 | tf_op jit(solution)/shard_map/ppermute | solution.py:298
  28.1 26.5 %collective-permute-start.13 = (bf16[2,128,512]{2,1,0:T(8,128)(2,1)S(1)}, bf16[2,128,512]{2,1,0:T(8,128)(2,1)}, u32[]{:S(2)}, u32[]{:S(2)}) collective-permute-start(bf16[2,128,512]{2,1,0:T(8,128)(2,1)S(1)} %pad_maximum_fusion.2.refs_6_), channel_id=1, source_target_pairs={{0,4},{1,5},{2,0},{3,1},{6,2},{7,3},{4,6},{5,7},{8,12},{9,13},{10,... | collective-permute-start | bytes 786440 | tf_op jit(solution)/shard_map/ppermute | solution.py:306
  30.1 24.5 %collective-permute-start.12 = (bf16[2,128,512]{2,1,0:T(8,128)(2,1)S(1)}, bf16[2,128,512]{2,1,0:T(8,128)(2,1)}, u32[]{:S(2)}, u32[]{:S(2)}) collective-permute-start(bf16[2,128,512]{2,1,0:T(8,128)(2,1)S(1)} %pad_maximum_fusion.2.refs_6_), channel_id=1, source_target_pairs={{0,6},{1,7},{2,4},{3,5},{6,0},{7,1},{4,2},{5,3},{8,14},{9,15},{10,... | collective-permute-start | bytes 786440 | tf_op jit(solution)/shard_map/ppermute | solution.py:306
  33.1 19.5 %collective-permute-start.9 = (bf16[2,128,512]{2,1,0:T(8,128)(2,1)S(1)}, bf16[2,128,512]{2,1,0:T(8,128)(2,1)S(1)}, u32[]{:S(2)}, u32[]{:S(2)}) collective-permute-start(bf16[2,128,512]{2,1,0:T(8,128)(2,1)S(1)} %pad_maximum_fusion.2.refs_6_), channel_id=1, source_target_pairs={{0,2},{1,3},{2,6},{3,7},{6,4},{7,5},{4,0},{5,1},{8,10},{9,11},{10,... | collective-permute-start | bytes 786440 | tf_op jit(solution)/shard_map/ppermute | solution.py:306
  42.4 0.7 copy-start.4
  43.1 0.7 copy-start.5
  43.8 15.8 %copy-start.3 = (bf16[1,128,2560]{2,1,0:T(8,128)(2,1)S(1)}, bf16[1,128,2560]{2,1,0:T(8,128)(2,1)}, u32[]{:S(2)}) copy-start(bf16[1,128,2560]{2,1,0:T(8,128)(2,1)} %refs_3_.3) | copy-start | bytes 1966084
  52.5 0.7 copy-start.6
  53.2 6.3 %collective-permute-start.11 = (bf16[2,128,1280]{2,1,0:T(8,128)(2,1)S(1)}, bf16[2,128,1280]{2,1,0:T(8,128)(2,1)}, u32[]{:S(2)}, u32[]{:S(2)}) collective-permute-start(bf16[2,128,1280]{2,1,0:T(8,128)(2,1)S(1)} %get-tuple-element.40), channel_id=1, source_target_pairs={{8,0},{16,8},{24,16},{9,1},{17,9},{25,17},{10,2},{18,10},{26,18},{... | collective-permute-start | bytes 1966088 | tf_op jit(solution)/shard_map/ppermute | solution.py:372
  54.5 5.0 %copy-start.7 = (bf16[2,128,512]{2,1,0:T(8,128)(2,1)S(1)}, bf16[2,128,512]{2,1,0:T(8,128)(2,1)}, u32[]{:S(2)}) copy-start(bf16[2,128,512]{2,1,0:T(8,128)(2,1)} %copy-done.6) | copy-start | bytes 786436
  54.6 14.2 %collective-permute-start.16 = (bf16[2,128,512]{2,1,0:T(8,128)(2,1)}, bf16[2,128,512]{2,1,0:T(8,128)(2,1)S(1)}, u32[]{:S(2)}, u32[]{:S(2)}) collective-permute-start(bf16[2,128,512]{2,1,0:T(8,128)(2,1)} %copy-done.5), channel_id=1, source_target_pairs={{0,4},{1,5},{2,0},{3,1},{6,2},{7,3},{4,6},{5,7},{8,12},{9,13},{10,... | collective-permute-start | bytes 786440 | tf_op jit(solution)/shard_map/ppermute | solution.py:306
  54.6 17.0 %collective-permute-start.17 = (bf16[2,128,512]{2,1,0:T(8,128)(2,1)}, bf16[2,128,512]{2,1,0:T(8,128)(2,1)S(1)}, u32[]{:S(2)}, u32[]{:S(2)}) collective-permute-start(bf16[2,128,512]{2,1,0:T(8,128)(2,1)} %copy-done.4), channel_id=1, source_target_pairs={{0,6},{1,7},{2,4},{3,5},{6,0},{7,1},{4,2},{5,3},{8,14},{9,15},{10,... | collective-permute-start | bytes 786440 | tf_op jit(solution)/shard_map/ppermute | solution.py:306
  56.9 35.4 %collective-permute-start.18 = (bf16[2,128,512]{2,1,0:T(8,128)(2,1)S(1)}, bf16[2,128,512]{2,1,0:T(8,128)(2,1)S(1)}, u32[]{:S(2)}, u32[]{:S(2)}) collective-permute-start(bf16[2,128,512]{2,1,0:T(8,128)(2,1)S(1)} %get-tuple-element.56), channel_id=1, source_target_pairs={{0,2},{1,3},{2,6},{3,7},{6,4},{7,5},{4,0},{5,1},{8,10},{9,11},{10,... | collective-permute-start | bytes 786440 | tf_op jit(solution)/shard_map/ppermute | solution.py:306
  58.0 35.8 %collective-permute-start.15 = (bf16[128,1280]{1,0:T(8,128)(2,1)S(1)}, bf16[128,1280]{1,0:T(8,128)(2,1)S(1)}, u32[]{:S(2)}, u32[]{:S(2)}) collective-permute-start(bf16[128,1280]{1,0:T(8,128)(2,1)S(1)} %get-tuple-element.73), channel_id=1, source_target_pairs={{0,1},{1,0},{2,3},{3,2},{4,5},{5,4},{6,7},{7,6},{8,9},{9,8},{10,11... | collective-permute-start | bytes 983048 | tf_op jit(solution)/shard_map/ppermute | solution.py:298
  68.3 25.5 %collective-permute-start.14 = (bf16[2,128,512]{2,1,0:T(8,128)(2,1)S(1)}, bf16[2,128,512]{2,1,0:T(8,128)(2,1)S(1)}, u32[]{:S(2)}, u32[]{:S(2)}) collective-permute-start(bf16[2,128,512]{2,1,0:T(8,128)(2,1)S(1)} %get-tuple-element.52), channel_id=1, source_target_pairs={{0,4},{1,5},{2,0},{3,1},{6,2},{7,3},{4,6},{5,7},{8,12},{9,13},{10,... | collective-permute-start | bytes 786440 | tf_op jit(solution)/shard_map/ppermute | solution.py:306
  68.7 25.8 %collective-permute-start.21 = (bf16[2,128,512]{2,1,0:T(8,128)(2,1)S(1)}, bf16[2,128,512]{2,1,0:T(8,128)(2,1)S(1)}, u32[]{:S(2)}, u32[]{:S(2)}) collective-permute-start(bf16[2,128,512]{2,1,0:T(8,128)(2,1)S(1)} %get-tuple-element.65), channel_id=1, source_target_pairs={{0,6},{1,7},{2,4},{3,5},{6,0},{7,1},{4,2},{5,3},{8,14},{9,15},{10,... | collective-permute-start | bytes 786440 | tf_op jit(solution)/shard_map/ppermute | solution.py:306
  71.6 31.9 %collective-permute-start.22 = (bf16[2,128,512]{2,1,0:T(8,128)(2,1)S(1)}, bf16[2,128,512]{2,1,0:T(8,128)(2,1)S(1)}, u32[]{:S(2)}, u32[]{:S(2)}) collective-permute-start(bf16[2,128,512]{2,1,0:T(8,128)(2,1)S(1)} %get-tuple-element.66), channel_id=1, source_target_pairs={{0,2},{1,3},{2,6},{3,7},{6,4},{7,5},{4,0},{5,1},{8,10},{9,11},{10,... | collective-permute-start | bytes 786440 | tf_op jit(solution)/shard_map/ppermute | solution.py:306
  92.3 14.0 %collective-permute-start.19 = (bf16[128,1280]{1,0:T(8,128)(2,1)S(1)}, bf16[128,1280]{1,0:T(8,128)(2,1)S(1)}, u32[]{:S(2)}, u32[]{:S(2)}) collective-permute-start(bf16[128,1280]{1,0:T(8,128)(2,1)S(1)} %get-tuple-element.71), channel_id=1, source_target_pairs={{0,1},{1,0},{2,3},{3,2},{4,5},{5,4},{6,7},{7,6},{8,9},{9,8},{10,11... | collective-permute-start | bytes 983048 | tf_op jit(solution)/shard_map/ppermute | solution.py:298
  94.0 13.3 %collective-permute-start.20 = (bf16[128,512]{1,0:T(8,128)(2,1)S(1)}, bf16[128,512]{1,0:T(8,128)(2,1)S(1)}, u32[]{:S(2)}, u32[]{:S(2)}) collective-permute-start(bf16[128,512]{1,0:T(8,128)(2,1)S(1)} %get-tuple-element.75), channel_id=1, source_target_pairs={{0,1},{1,0},{2,3},{3,2},{4,5},{5,4},{6,7},{7,6},{8,9},{9,8},{10,11... | collective-permute-start | bytes 393224 | tf_op jit(solution)/shard_map/ppermute | solution.py:298
  103.7 5.6 %collective-permute-start.23 = (bf16[128,512]{1,0:T(8,128)(2,1)S(1)}, bf16[128,512]{1,0:T(8,128)(2,1)S(1)}, u32[]{:S(2)}, u32[]{:S(2)}) collective-permute-start(bf16[128,512]{1,0:T(8,128)(2,1)S(1)} %get-tuple-element.77), channel_id=1, source_target_pairs={{0,1},{1,0},{2,3},{3,2},{4,5},{5,4},{6,7},{7,6},{8,9},{9,8},{10,11... | collective-permute-start | bytes 393224 | tf_op jit(solution)/shard_map/ppermute | solution.py:298
